TPU v7x, 128 devices: a whole 4x4x4 slice. The times are simulated.
128 devices in a mesh: frame: 8 (over z, y_lo), height: 8 (over y_hi, x), head: 2 (over core).
Axes of the slice: x: 4, y: 4 (y_hi: 2, y_lo: 2; y = y_hi * 2 + y_lo), z: 4, core: 2. Of those that a mesh axis runs over, the one named last changes fastest.
Arguments:
- queries: bfloat16 [16, 64, 48, 2560], P(('frame', 'head'), 'height'), may hold values from -112 to 112
- keys: bfloat16 [16, 64, 48, 2560], P(('frame', 'head'), 'height'), may hold values from -4 to 4
- values: bfloat16 [16, 64, 48, 2560], P(('frame', 'head'), 'height'), may hold values from -6 to 6
- out_weight: bfloat16 [2560, 5120], P('head'), may hold values from -0.25 to 0.25
- window_radii: int32 [20, 3], replicated, may hold values from 0 to 1
- frame_valid: int32 [16], replicated, may hold values from 0 to 1, as said below
Outputs:
- projected: bfloat16 [16, 64, 48, 5120], P(('frame', 'head'), 'height')
Inputs may be any that keep to these rules, and one draw needn't show every extreme that they name: `frame_valid`: padding frames form a run of 0 to 2 frames at the start and a run of 1 to 2 frames at the end.
All inputs are finite; a program needn't handle non-finite values.
Results may differ from a plain program's by a relative error of at most 0.0057.
Values may be sent and summed in bfloat16 or wider, within the bound.
No kernel may reach another device: no remote copies, remote signals or barrier semaphores. Data moves between devices by JAX's collectives and lax.ppermute only.
A program may use at most 192 MiB of HBM per device.

v0:
```python
import jax
import jax.numpy as jnp
from jax import lax
from jax.sharding import PartitionSpec as P

HEAD_DIM = 128
ROW_TILE = 2
COL_TILE = 16


NEG_FILL = -1e30


def padded(block, sides, width):
    for axis, dim in sides:
        count = lax.axis_size(axis)
        forward = [(i, i + 1) for i in range(count - 1)]
        backward = [(target, source) for source, target in forward]
        low = lax.ppermute(
            lax.slice_in_dim(block, block.shape[dim] - width, None, axis=dim), axis, forward
        )
        high = lax.ppermute(lax.slice_in_dim(block, 0, width, axis=dim), axis, backward)
        block = jnp.concatenate([low, block, high], axis=dim)
    return block


def head_major(tensor, local_heads, row_tiles_dev, block_queries):
    frames_dev, rows_dev, col_total, local_width = tensor.shape
    split = tensor.reshape(frames_dev, rows_dev * col_total, local_heads, HEAD_DIM)
    moved = split.transpose(2, 0, 1, 3)
    return moved.reshape(local_heads, frames_dev, row_tiles_dev, block_queries, HEAD_DIM)


def on_device(queries, keys, values, out_weight, window_radii, frame_valid):
    head_parts = lax.axis_size("head")
    local_query, local_key, local_value = (
        lax.all_to_all(queries, "head", split_axis=3, concat_axis=0, tiled=True),
        lax.all_to_all(keys, "head", split_axis=3, concat_axis=0, tiled=True),
        lax.all_to_all(values, "head", split_axis=3, concat_axis=0, tiled=True),
    )
    frames_dev, rows_dev, col_total, local_width = local_query.shape
    local_heads = local_width // HEAD_DIM
    row_tiles_dev = rows_dev // ROW_TILE
    block_queries = ROW_TILE * col_total
    block_keys = 9 * block_queries
    query_count = frames_dev * rows_dev * col_total
    query_heads = head_major(local_query, local_heads, row_tiles_dev, block_queries)
    stacked = jnp.stack(
        (
            head_major(local_key, local_heads, row_tiles_dev, block_queries),
            head_major(local_value, local_heads, row_tiles_dev, block_queries),
        ),
        0,
    )
    widened = padded(stacked, (("frame", 2), ("height", 3)), 1)
    ext_frames = frames_dev + 2
    frame_first = lax.axis_index("frame") * frames_dev
    tile_first = lax.axis_index("height") * row_tiles_dev
    tile_total = row_tiles_dev * lax.axis_size("height")
    head_first = lax.axis_index("head") * local_heads
    radii_local = lax.dynamic_slice_in_dim(window_radii, head_first, local_heads, 0)
    valid_pad = jnp.pad(frame_valid, (1, 1))
    valid_ext = lax.dynamic_slice_in_dim(valid_pad, frame_first, ext_frames, 0)
    offsets = jnp.arange(3, dtype=jnp.int32)
    key_index = jnp.arange(block_keys, dtype=jnp.int32)
    key_frame = key_index // (3 * block_queries)
    key_tile = key_index // block_queries % 3
    key_col = key_index % col_total // COL_TILE
    query_col = jnp.arange(block_queries, dtype=jnp.int32) % col_total // COL_TILE
    col_gap = jnp.abs(query_col[:, None] - key_col[None, :])
    col_allow = col_gap[None] <= radii_local[:, 2][:, None, None]
    frame_near = jnp.abs(key_frame - 1)[None] <= radii_local[:, 0:1]
    tile_near = jnp.abs(key_tile - 1)[None] <= radii_local[:, 1:2]
    frame_pick = key_frame[None, :] == offsets[:, None]
    tile_pick = key_tile[None, :] == offsets[:, None]

    def one_block(block):
        frame_at = block // row_tiles_dev
        tile_at = block % row_tiles_dev
        query_rows = lax.dynamic_slice(
            query_heads, (0, frame_at, tile_at, 0, 0), (local_heads, 1, 1, block_queries, HEAD_DIM)
        ).reshape(local_heads, block_queries, HEAD_DIM)
        slab = lax.dynamic_slice(
            widened,
            (0, 0, frame_at, tile_at, 0, 0),
            (2, local_heads, 3, 3, block_queries, HEAD_DIM),
        ).reshape(2, local_heads, block_keys, HEAD_DIM)
        valid_three = lax.dynamic_slice_in_dim(valid_ext, frame_at, 3, 0)
        frame_ok = (valid_three == 1) | (offsets == 1)
        tile_global = tile_first + tile_at + offsets - 1
        tile_exists = (tile_global >= 0) & (tile_global < tile_total)
        frame_key_ok = jnp.any(frame_pick & frame_ok[:, None], axis=0)
        tile_key_ok = jnp.any(tile_pick & tile_exists[:, None], axis=0)
        key_allow = frame_near & tile_near & (frame_key_ok & tile_key_ok)[None]
        allowed = key_allow[:, None, :] & col_allow
        scores = jnp.einsum(
            "hqd,hkd->hqk", query_rows, slab[0], preferred_element_type=jnp.float32
        ) * HEAD_DIM ** (-0.5)
        masked = jnp.where(allowed, scores, NEG_FILL)
        highest = jnp.max(masked, axis=2, keepdims=True)
        expo = jnp.exp(masked - highest)
        probs = (expo / jnp.sum(expo, axis=2, keepdims=True)).astype(jnp.bfloat16)
        return jnp.einsum(
            "hqk,hkd->hqd", probs, slab[1], preferred_element_type=jnp.float32
        ).astype(jnp.bfloat16)

    block_total = frames_dev * row_tiles_dev
    per_block = lax.map(one_block, jnp.arange(block_total, dtype=jnp.int32))
    attended = per_block.transpose(0, 2, 1, 3)
    attended = attended.reshape(query_count, local_width)
    summed = lax.psum_scatter(
        jnp.dot(attended, out_weight, preferred_element_type=jnp.float32),
        "head",
        scatter_dimension=0,
        tiled=True,
    )
    return summed.astype(jnp.bfloat16).reshape(
        frames_dev // head_parts, rows_dev, col_total, out_weight.shape[1]
    )


def solution(mesh):
    return jax.shard_map(
        on_device,
        mesh=mesh,
        in_specs=(
            P(("frame", "head"), "height", None, None),
            P(("frame", "head"), "height", None, None),
            P(("frame", "head"), "height", None, None),
            P("head", None),
            P(),
            P(),
        ),
        out_specs=P(("frame", "head"), "height", None, None),
        check_vma=False,
    )
```

profile of v0, /device:TPU:1, one launch (start us, length us, event | category | flops | bytes accessed | tf_op | source)
XLA Modules:
  0.0 448.1 jit_solution(5983245406564591680)
XLA Ops:
  6.5 6.7 %copy.29 = bf16[1,8,48,2560]{2,1,0,3:T(8,128)(2,1)} copy(bf16[1,8,48,2560]{3,2,1,0:T(8,128)(2,1)} %param.9) | data formatting | bytes 3932160 | tf_op args[1]
  13.3 10.4 %reshape.268 = bf16[2,2,245760]{2,1,0:T(2,128)(2,1)} reshape(bf16[2560,1,8,48]{3,2,1,0:T(8,128)(2,1)} %bitcast.89) | data formatting | bytes 3932160
  23.7 5.2 %all-to-all-start.1 = ((bf16[2,2,245760]{2,1,0:T(2,128)(2,1)}), bf16[2,2,245760]{2,1,0:T(2,128)(2,1)S(1)}, u32[]{:S(2)}, u32[]{:S(2)}) async-start(bf16[2,2,245760]{2,1,0:T(2,128)(2,1)} %reshape.268), calls=%async_computation.1 | async-start | bytes 3932160 | tf_op jit(solution)/shard_map/all_to_all | solution.py:38
  28.8 6.8 %copy.31 = bf16[1,8,48,2560]{2,1,0,3:T(8,128)(2,1)} copy(bf16[1,8,48,2560]{3,2,1,0:T(8,128)(2,1)} %param.10) | data formatting | bytes 3932160 | tf_op args[2]
  35.6 10.4 %reshape.270 = bf16[2,2,245760]{2,1,0:T(2,128)(2,1)} reshape(bf16[2560,1,8,48]{3,2,1,0:T(8,128)(2,1)} %bitcast.90) | data formatting | bytes 3932160
  46.1 5.3 %all-to-all-start.2 = ((bf16[2,2,245760]{2,1,0:T(2,128)(2,1)}), bf16[2,2,245760]{2,1,0:T(2,128)(2,1)}, u32[]{:S(2)}, u32[]{:S(2)}) async-start(bf16[2,2,245760]{2,1,0:T(2,128)(2,1)} %reshape.270), calls=%async_computation.2 | async-start | bytes 3932160 | tf_op jit(solution)/shard_map/all_to_all | solution.py:39
  51.4 7.0 %reshape.269 = bf16[2560,1,8,48]{3,2,1,0:T(8,128)(2,1)} reshape(bf16[2,2,245760]{2,1,0:T(2,128)(2,1)S(1)} %all-to-all-done.1) | data formatting | bytes 3932160
  58.4 6.2 %copy.30 = bf16[1,8,48,2,1280]{4,2,1,3,0:T(8,128)(2,1)} copy(bf16[1,8,48,2,1280]{2,1,4,3,0:T(8,128)(2,1)} %bitcast.86) | data formatting | bytes 3932160 | tf_op jit(solution)/shard_map/all_to_all | solution.py:38
  64.6 3.7 reshape.260
  68.3 1.8 copy_dynamic-update-slice_fusion.1
  70.1 7.5 %reshape.271 = bf16[2560,1,8,48]{3,2,1,0:T(8,128)(2,1)} reshape(bf16[2,2,245760]{2,1,0:T(2,128)(2,1)} %all-to-all-done.2) | data formatting | bytes 3932160
  77.6 6.3 %copy.32 = bf16[1,8,48,2,1280]{4,2,1,3,0:T(8,128)(2,1)} copy(bf16[1,8,48,2,1280]{2,1,4,3,0:T(8,128)(2,1)} %bitcast.87) | data formatting | bytes 3932160 | tf_op jit(solution)/shard_map/all_to_all | solution.py:39
  83.9 3.7 reshape.261
  87.7 1.8 copy_dynamic-update-slice_fusion
  89.5 3.0 fusion.57
  92.4 3.4 collective-permute-start
  95.9 1.4 collective-permute-start.1
  97.3 40.7 %collective-permute-done = bf16[2,10,1,4,96,128]{5,4,3,2,1,0:T(8,128)(2,1)S(1)} collective-permute-done((bf16[2,10,1,4,96,128]{5,4,3,2,1,0:T(8,128)(2,1)S(1)}, bf16[2,10,1,4,96,128]{5,4,3,2,1,0:T(8,128)(2,1)S(1)}, u32[]{:S(2)}, u32[]{:S(2)}) %collective-permute-start) | collective-permute-done | bytes 1966112 | tf_op jit(solution)/shard_map/ppermute | solution.py:19
  138.0 44.4 %collective-permute-done.1 = bf16[2,10,1,4,96,128]{5,4,3,2,1,0:T(8,128)(2,1)S(1)} collective-permute-done((bf16[2,10,1,4,96,128]{5,4,3,2,1,0:T(8,128)(2,1)S(1)}, bf16[2,10,1,4,96,128]{5,4,3,2,1,0:T(8,128)(2,1)S(1)}, u32[]{:S(2)}, u32[]{:S(2)}) %collective-permute-start.1) | collective-permute-done | bytes 1966112 | tf_op jit(solution)/shard_map/ppermute | solution.py:22
  182.4 2.2 pad_maximum_fusion.3
  184.9 4.4 collective-permute-start.2
  189.3 1.5 collective-permute-start.3
  190.8 5.3 %copy.26 = bf16[1,8,48,2560]{2,1,0,3:T(8,128)(2,1)} copy(bf16[1,8,48,2560]{3,2,1,0:T(8,128)(2,1)S(1)} %copy-done.5) | data formatting | bytes 3932160 | tf_op args[0]
  196.1 10.4 %reshape.266 = bf16[2,2,245760]{2,1,0:T(2,128)(2,1)} reshape(bf16[2560,1,8,48]{3,2,1,0:T(8,128)(2,1)} %bitcast.91) | data formatting | bytes 3932160
  206.5 4.7 %all-to-all-start = ((bf16[2,2,245760]{2,1,0:T(2,128)(2,1)}), bf16[2,2,245760]{2,1,0:T(2,128)(2,1)S(1)}, u32[]{:S(2)}, u32[]{:S(2)}) async-start(bf16[2,2,245760]{2,1,0:T(2,128)(2,1)} %reshape.266), calls=%async_computation | async-start | bytes 3932160 | tf_op jit(solution)/shard_map/all_to_all | solution.py:37
  211.3 2.4 all-to-all-done
  213.7 7.0 %reshape.267 = bf16[2560,1,8,48]{3,2,1,0:T(8,128)(2,1)} reshape(bf16[2,2,245760]{2,1,0:T(2,128)(2,1)S(1)} %all-to-all-done) | data formatting | bytes 3932160
  220.7 6.2 %copy.27 = bf16[1,8,48,2,1280]{4,2,1,3,0:T(8,128)(2,1)} copy(bf16[1,8,48,2,1280]{2,1,4,3,0:T(8,128)(2,1)} %bitcast.88) | data formatting | bytes 3932160 | tf_op jit(solution)/shard_map/all_to_all | solution.py:37
  226.9 3.7 reshape.258
  230.7 1.8 copy.35
  232.8 2.0 collective-permute-done.3
  234.8 10.3 %pad_maximum_fusion = bf16[2,10,4,6,96,128]{5,4,3,2,1,0:T(8,128)(2,1)} fusion(bf16[2,10,4,1,96,128]{5,4,3,2,1,0:T(8,128)(2,1)} %collective-permute-done.3, bf16[2,10,1,4,96,128]{5,4,3,2,1,0:T(8,128)(2,1)} %copy-done.4, bf16[2,10,2,4,96,128]{5,4,3,2,1,0:T(8,128)(2,1)} %copy_dynamic-update-slice_fusion, bf16[2,10,1,4,96,128]{5,4,3,2,1,0:T(8,128)(2,1)} %copy-done.3, ...), kind=kLoop, calls=%fused_computation.43 | loop fusion | flops 23592960 | bytes 23592960 | tf_op jit(solution)/shard_map/concatenate | solution.py:23
  245.1 133.1 %while.15 = (s32[]{:T(128)}, bf16[8,10,96,128]{3,2,1,0:T(8,128)(2,1)}, s32[8]{0:T(128)S(1)}, s32[4]{0:T(128)S(1)}, s32[]{:T(128)}, /*index=5*/bf16[10,2,4,96,128...) while((s32[]{:T(128)}, ...), condition=%wide.region_5.6_spmd.clone.clone, body=%wide.region_0.5_spmd.clone.clone.sunk | while | flops 431481856 | bytes 20897932 | solution.py:108
  245.1 0.6 dynamic_slice.64
  248.3 4.5 constant_dynamic-slice_fusion.4
  253.1 5.3 %fusion.73 = (f32[10,96]{1,0:T(8,128)S(1)}, f32[10,96,864]{2,1,0:T(8,128)}) fusion(s32[96,864]{1,0:T(8,128)S(1)} %get-tuple-element.539, s32[10]{0:T(128)S(1)} %get-tuple-element.538, pred[10,864]{1,0:T(8,128)(4,1)S(1)} %bitcast_and_fusion.2, bf16[10,864,128]{2,1,0:T(8,128)(2,1)} %bitcast.85, bf16[10,2,4,96,128]{4,3,0,2,1:T(8,128)(2,1)} %get-tuple-element.530, ...), kind=kOutput, calls=%fused_computation.89.clone.1 | convolution fusion | flops 217314144 | bytes 6119664 | tf_op jit(solution)/shard_map/while/body/eval_jaxpr/sub | solution.py:101
  258.4 3.4 fusion.74
  261.8 0.6 dynamic_slice.64
  265.0 4.5 constant_dynamic-slice_fusion.4
  269.7 5.3 %fusion.73 = (f32[10,96]{1,0:T(8,128)S(1)}, f32[10,96,864]{2,1,0:T(8,128)}) fusion(s32[96,864]{1,0:T(8,128)S(1)} %get-tuple-element.539, s32[10]{0:T(128)S(1)} %get-tuple-element.538, pred[10,864]{1,0:T(8,128)(4,1)S(1)} %bitcast_and_fusion.2, bf16[10,864,128]{2,1,0:T(8,128)(2,1)} %bitcast.85, bf16[10,2,4,96,128]{4,3,0,2,1:T(8,128)(2,1)} %get-tuple-element.530, ...), kind=kOutput, calls=%fused_computation.89.clone.1 | convolution fusion | flops 217314144 | bytes 6119664 | tf_op jit(solution)/shard_map/while/body/eval_jaxpr/sub | solution.py:101
  275.0 3.4 fusion.74
  281.6 4.5 constant_dynamic-slice_fusion.4
  286.4 5.3 %fusion.73 = (f32[10,96]{1,0:T(8,128)S(1)}, f32[10,96,864]{2,1,0:T(8,128)}) fusion(s32[96,864]{1,0:T(8,128)S(1)} %get-tuple-element.539, s32[10]{0:T(128)S(1)} %get-tuple-element.538, pred[10,864]{1,0:T(8,128)(4,1)S(1)} %bitcast_and_fusion.2, bf16[10,864,128]{2,1,0:T(8,128)(2,1)} %bitcast.85, bf16[10,2,4,96,128]{4,3,0,2,1:T(8,128)(2,1)} %get-tuple-element.530, ...), kind=kOutput, calls=%fused_computation.89.clone.1 | convolution fusion | flops 217314144 | bytes 6119664 | tf_op jit(solution)/shard_map/while/body/eval_jaxpr/sub | solution.py:101
  291.6 3.4 fusion.74
  298.2 4.5 constant_dynamic-slice_fusion.4
  303.0 5.2 %fusion.73 = (f32[10,96]{1,0:T(8,128)S(1)}, f32[10,96,864]{2,1,0:T(8,128)}) fusion(s32[96,864]{1,0:T(8,128)S(1)} %get-tuple-element.539, s32[10]{0:T(128)S(1)} %get-tuple-element.538, pred[10,864]{1,0:T(8,128)(4,1)S(1)} %bitcast_and_fusion.2, bf16[10,864,128]{2,1,0:T(8,128)(2,1)} %bitcast.85, bf16[10,2,4,96,128]{4,3,0,2,1:T(8,128)(2,1)} %get-tuple-element.530, ...), kind=kOutput, calls=%fused_computation.89.clone.1 | convolution fusion | flops 217314144 | bytes 6119664 | tf_op jit(solution)/shard_map/while/body/eval_jaxpr/sub | solution.py:101
  308.3 3.4 fusion.74
  314.9 4.5 constant_dynamic-slice_fusion.4
  319.6 5.3 %fusion.73 = (f32[10,96]{1,0:T(8,128)S(1)}, f32[10,96,864]{2,1,0:T(8,128)}) fusion(s32[96,864]{1,0:T(8,128)S(1)} %get-tuple-element.539, s32[10]{0:T(128)S(1)} %get-tuple-element.538, pred[10,864]{1,0:T(8,128)(4,1)S(1)} %bitcast_and_fusion.2, bf16[10,864,128]{2,1,0:T(8,128)(2,1)} %bitcast.85, bf16[10,2,4,96,128]{4,3,0,2,1:T(8,128)(2,1)} %get-tuple-element.530, ...), kind=kOutput, calls=%fused_computation.89.clone.1 | convolution fusion | flops 217314144 | bytes 6119664 | tf_op jit(solution)/shard_map/while/body/eval_jaxpr/sub | solution.py:101
  324.9 3.4 fusion.74
  331.5 4.5 constant_dynamic-slice_fusion.4
  336.3 5.3 %fusion.73 = (f32[10,96]{1,0:T(8,128)S(1)}, f32[10,96,864]{2,1,0:T(8,128)}) fusion(s32[96,864]{1,0:T(8,128)S(1)} %get-tuple-element.539, s32[10]{0:T(128)S(1)} %get-tuple-element.538, pred[10,864]{1,0:T(8,128)(4,1)S(1)} %bitcast_and_fusion.2, bf16[10,864,128]{2,1,0:T(8,128)(2,1)} %bitcast.85, bf16[10,2,4,96,128]{4,3,0,2,1:T(8,128)(2,1)} %get-tuple-element.530, ...), kind=kOutput, calls=%fused_computation.89.clone.1 | convolution fusion | flops 217314144 | bytes 6119664 | tf_op jit(solution)/shard_map/while/body/eval_jaxpr/sub | solution.py:101
  341.5 3.4 fusion.74
  348.1 4.5 constant_dynamic-slice_fusion.4
  352.9 5.2 %fusion.73 = (f32[10,96]{1,0:T(8,128)S(1)}, f32[10,96,864]{2,1,0:T(8,128)}) fusion(s32[96,864]{1,0:T(8,128)S(1)} %get-tuple-element.539, s32[10]{0:T(128)S(1)} %get-tuple-element.538, pred[10,864]{1,0:T(8,128)(4,1)S(1)} %bitcast_and_fusion.2, bf16[10,864,128]{2,1,0:T(8,128)(2,1)} %bitcast.85, bf16[10,2,4,96,128]{4,3,0,2,1:T(8,128)(2,1)} %get-tuple-element.530, ...), kind=kOutput, calls=%fused_computation.89.clone.1 | convolution fusion | flops 217314144 | bytes 6119664 | tf_op jit(solution)/shard_map/while/body/eval_jaxpr/sub | solution.py:101
  358.2 3.4 fusion.74
  364.8 4.5 constant_dynamic-slice_fusion.4
  369.5 5.2 %fusion.73 = (f32[10,96]{1,0:T(8,128)S(1)}, f32[10,96,864]{2,1,0:T(8,128)}) fusion(s32[96,864]{1,0:T(8,128)S(1)} %get-tuple-element.539, s32[10]{0:T(128)S(1)} %get-tuple-element.538, pred[10,864]{1,0:T(8,128)(4,1)S(1)} %bitcast_and_fusion.2, bf16[10,864,128]{2,1,0:T(8,128)(2,1)} %bitcast.85, bf16[10,2,4,96,128]{4,3,0,2,1:T(8,128)(2,1)} %get-tuple-element.530, ...), kind=kOutput, calls=%fused_computation.89.clone.1 | convolution fusion | flops 217314144 | bytes 6119664 | tf_op jit(solution)/shard_map/while/body/eval_jaxpr/sub | solution.py:101
  374.8 3.4 fusion.74
  378.2 3.7 copy.36
  381.9 3.1 reshape.262
  385.0 17.4 %fusion.58 = f32[768,5120]{1,0:T(8,128)} fusion(bf16[768,1280]{0,1:T(8,128)(2,1)} %reshape.262, bf16[1280,5120]{1,0:T(8,128)(2,1)} %param.11), kind=kOutput, calls=%fused_computation.91 | convolution fusion | flops 10066329600 | bytes 30801920 | tf_op jit(solution)/shard_map/dot_general | solution.py:112
  402.4 32.8 %reduce-scatter.2.cloned.1.call-done = f32[384,5120]{1,0:T(8,128)} async-done(((f32[768,5120]{1,0:T(8,128)}), f32[384,5120]{1,0:T(8,128)}) %reduce-scatter.2.cloned.1.call-update) | async-done | bytes 7864336 | tf_op jit(solution)/shard_map/reduce_scatter | solution.py:111
  435.3 5.7 %convert_element_type.17 = bf16[384,5120]{1,0:T(8,128)(2,1)} convert(f32[384,5120]{1,0:T(8,128)} %reduce-scatter.2.cloned.1.call-done) | non-fusion elementwise | flops 1966080 | bytes 11796480 | tf_op jit(solution)/shard_map/convert_element_type | solution.py:117
  (75 shorter events, 6.4 us)
Async XLA Ops:
  6.5 226.0 %copy-start = (s32[20,3]{0,1:T(4,128)S(1)}, s32[20,3]{0,1:T(4,128)}, u32[]{:S(2)}) copy-start(s32[20,3]{0,1:T(4,128)} %param.12) | copy-start | bytes 724
  23.7 22.4 %all-to-all-start.1 = ((bf16[2,2,245760]{2,1,0:T(2,128)(2,1)}), bf16[2,2,245760]{2,1,0:T(2,128)(2,1)S(1)}, u32[]{:S(2)}, u32[]{:S(2)}) async-start(bf16[2,2,245760]{2,1,0:T(2,128)(2,1)} %reshape.268), calls=%async_computation.1 | async-start | bytes 3932160 | tf_op jit(solution)/shard_map/all_to_all | solution.py:38
  46.1 24.0 %all-to-all-start.2 = ((bf16[2,2,245760]{2,1,0:T(2,128)(2,1)}), bf16[2,2,245760]{2,1,0:T(2,128)(2,1)}, u32[]{:S(2)}, u32[]{:S(2)}) async-start(bf16[2,2,245760]{2,1,0:T(2,128)(2,1)} %reshape.270), calls=%async_computation.2 | async-start | bytes 3932160 | tf_op jit(solution)/shard_map/all_to_all | solution.py:39
  89.5 92.9 %copy-start.2 = (bf16[2,10,2,4,96,128]{5,4,3,2,1,0:T(8,128)(2,1)S(1)}, bf16[2,10,2,4,96,128]{5,4,3,2,1,0:T(8,128)(2,1)}, u32[]{:S(2)}) copy-start(bf16[2,10,2,4,96,128]{5,4,3,2,1,0:T(8,128)(2,1)} %copy_dynamic-update-slice_fusion) | copy-start | bytes 11796484
  92.4 45.6 %collective-permute-start = (bf16[2,10,1,4,96,128]{5,4,3,2,1,0:T(8,128)(2,1)S(1)}, bf16[2,10,1,4,96,128]{5,4,3,2,1,0:T(8,128)(2,1)S(1)}, u32[]{:S(2)}, u32[]{:S(2)}) collective-permute-start(bf16[2,10,1,4,96,128]{5,4,3,2,1,0:T(8,128)(2,1)S(1)} %get-tuple-element.367), channel_id=1, source_target_pairs={{0,16},{16,32},{32,48},{48,64},{64,80},{80,96},{96,112},{1,17},{17... | collective-permute-start | bytes 5898248 | tf_op jit(solution)/shard_map/ppermute | solution.py:19
  95.9 94.9 %copy-start.5 = (bf16[1,8,48,2560]{3,2,1,0:T(8,128)(2,1)S(1)}, bf16[1,8,48,2560]{3,2,1,0:T(8,128)(2,1)}, u32[]{:S(2)}) copy-start(bf16[1,8,48,2560]{3,2,1,0:T(8,128)(2,1)} %param.8) | copy-start | bytes 5898244
  95.9 86.5 %collective-permute-start.1 = (bf16[2,10,1,4,96,128]{5,4,3,2,1,0:T(8,128)(2,1)S(1)}, bf16[2,10,1,4,96,128]{5,4,3,2,1,0:T(8,128)(2,1)S(1)}, u32[]{:S(2)}, u32[]{:S(2)}) collective-permute-start(bf16[2,10,1,4,96,128]{5,4,3,2,1,0:T(8,128)(2,1)S(1)} %get-tuple-element.368), channel_id=1, source_target_pairs={{16,0},{32,16},{48,32},{64,48},{80,64},{96,80},{112,96},{17,1},{33... | collective-permute-start | bytes 5898248 | tf_op jit(solution)/shard_map/ppermute | solution.py:22
  138.0 46.6 %copy-start.3 = (bf16[2,10,1,4,96,128]{5,4,3,2,1,0:T(8,128)(2,1)}, bf16[2,10,1,4,96,128]{5,4,3,2,1,0:T(8,128)(2,1)S(1)}, u32[]{:S(2)}) copy-start(bf16[2,10,1,4,96,128]{5,4,3,2,1,0:T(8,128)(2,1)S(1)} %collective-permute-done) | copy-start | bytes 5898244
  182.4 2.5 copy-start.4
  184.9 47.9 %collective-permute-start.2 = (bf16[2,10,4,1,96,128]{5,4,3,2,1,0:T(8,128)(2,1)}, bf16[2,10,4,1,96,128]{5,4,3,2,1,0:T(8,128)(2,1)}, u32[]{:S(2)}, u32[]{:S(2)}) collective-permute-start(bf16[2,10,4,1,96,128]{5,4,3,2,1,0:T(8,128)(2,1)} %get-tuple-element.365), channel_id=1, source_target_pairs={{0,2},{2,4},{4,6},{6,8},{8,10},{10,12},{12,14},{1,3},{3,5},{5,7},{... | collective-permute-start | bytes 5898248 | tf_op jit(solution)/shard_map/ppermute | solution.py:19
  189.3 45.5 %collective-permute-start.3 = (bf16[2,10,4,1,96,128]{5,4,3,2,1,0:T(8,128)(2,1)}, bf16[2,10,4,1,96,128]{5,4,3,2,1,0:T(8,128)(2,1)}, u32[]{:S(2)}, u32[]{:S(2)}) collective-permute-start(bf16[2,10,4,1,96,128]{5,4,3,2,1,0:T(8,128)(2,1)} %get-tuple-element.366), channel_id=1, source_target_pairs={{2,0},{4,2},{6,4},{8,6},{10,8},{12,10},{14,12},{3,1},{5,3},{7,5},{... | collective-permute-start | bytes 5898248 | tf_op jit(solution)/shard_map/ppermute | solution.py:22
  206.5 7.1 %all-to-all-start = ((bf16[2,2,245760]{2,1,0:T(2,128)(2,1)}), bf16[2,2,245760]{2,1,0:T(2,128)(2,1)S(1)}, u32[]{:S(2)}, u32[]{:S(2)}) async-start(bf16[2,2,245760]{2,1,0:T(2,128)(2,1)} %reshape.266), calls=%async_computation | async-start | bytes 3932160 | tf_op jit(solution)/shard_map/all_to_all | solution.py:37
  211.2 224.0 %reduce-scatter.2.cloned.1.call-start = ((), (), s32[]{:S(2)}) async-start(), calls=%async_computation.4 | async-start | bytes 23592960 | tf_op jit(solution)/shard_map/reduce_scatter | solution.py:111
  230.6 1.8 copy-start.6
  435.3 5.7 %copy-start.1 = (s32[20,3]{0,1:T(4,128)S(1)}, s32[20,3]{0,1:T(4,128)}, u32[]{:S(2)}) copy-start(s32[20,3]{0,1:T(4,128)} %param.12) | copy-start | bytes 724
Sparse Core Ops, SparseCore 0:
  402.6 32.6 reduce-scatter.1
where the time goes:
time: 457 us; the launch traced here: 448 us
  local copies, waits for them, and re-layouts  157 us (34%)
  waiting for transfers between devices  122 us (27%)
  matrix products  86.6 us (19%)
  starting transfers between devices  25.9 us (6%)
  loops' own time  21.2 us (5%)
  other arithmetic  20.7 us (5%)
  between operations  13.8 us (3%)
    unnamed x25, local copies, waits for them, and re-layouts  75.5 us
    ppermute x2, waiting for transfers between devices, padded(): lax.ppermute(lax.slice_in_dim(block, 0, width, axis=dim), axis, backward)  46.4 us
    sub x8, matrix products, one_block(): expo = jnp.exp(masked - highest)  42 us
    ppermute x2, waiting for transfers between devices, padded(): lax.ppermute(lax.slice_in_dim(block, block.shape[dim] - width, None, axis...  40.7 us
    slice x8, local copies, waits for them, and re-layouts, one_block(): slab[0]  35.7 us
    reduce_scatter x1, waiting for transfers between devices, on_device(): lax.psum_scatter(jnp.dot(attended, out_weight, preferred_element_type=jnp...  32.8 us
    dot_general x8, matrix products, one_block(): jnp.einsum('hqk,hkd->hqd', probs, slab[1], preferred_element_type=jnp.flo...  27.2 us
    another operation x1, loops' own time, on_device(): per_block = lax.map(one_block, jnp.arange(block_total, dtype=jnp.int32))  21.2 us
  transfers between devices with their start and end apart: 8, of which 5 were waited for; matrix products, arithmetic and copies ran while one was open for 16% of the time, Pallas kernels for 0%

commit v1 on v0

v1 whole, which is shorter than its diff:
```python
import functools
import math

import jax
import jax.numpy as jnp
import numpy as np
from jax import lax
from jax.experimental import pallas as pl
from jax.experimental.pallas import tpu as pltpu
from jax.sharding import PartitionSpec as P

HEAD_DIM = 128
ROW_TILE = 2
COL_TILE = 16
NEG_FILL = -1e30
GRID_AXES = ("frame", "head")
VMEM_BYTES = 56 * 1024 * 1024
SCALE = HEAD_DIM ** -0.5 * math.log2(math.e)


def copy_columns(order, sources, count, row_sets):
    def kernel(order_ref, *refs):
        ins, outs, sem = refs[: len(sources)], refs[len(sources) : -1], refs[-1]

        def copies(slot):
            columns = pl.ds(pl.multiple_of(order_ref[slot] * HEAD_DIM, HEAD_DIM), HEAD_DIM)
            for out, (start, rows) in zip(outs, row_sets):
                for which, source in enumerate(ins):
                    yield pltpu.make_async_copy(
                        source.at[pl.ds(start, rows), columns], out.at[slot, which], sem
                    )

        def begin(slot, carry):
            for copy in copies(slot):
                copy.start()
            return carry

        def end(slot, carry):
            for copy in copies(slot):
                copy.wait()
            return carry

        lax.fori_loop(0, count, begin, 0)
        lax.fori_loop(0, count, end, 0)

    return pl.pallas_call(
        kernel,
        out_shape=[
            jax.ShapeDtypeStruct((count, len(sources), rows, HEAD_DIM), sources[0].dtype)
            for _, rows in row_sets
        ],
        in_specs=[pl.BlockSpec(memory_space=pltpu.SMEM)]
        + [pl.BlockSpec(memory_space=pl.ANY)] * len(sources),
        out_specs=[pl.BlockSpec(memory_space=pl.ANY)] * len(row_sets),
        scratch_shapes=[pltpu.SemaphoreType.DMA],
    )(order, *sources)


def attend(query, keys, values, mask):
    scores = lax.dot_general(
        query, keys, (((1,), (1,)), ((), ())), preferred_element_type=jnp.float32
    )
    scores = scores * SCALE + mask
    highest = jnp.max(scores, axis=1, keepdims=True)
    expo = jnp.exp2(scores - highest)
    probs = expo * (1.0 / jnp.sum(expo, axis=1, keepdims=True))
    out = jnp.dot(probs.astype(jnp.bfloat16), values, preferred_element_type=jnp.float32)
    return out.astype(jnp.bfloat16)


def attention(meta, flags, key_info, query_col, qkv, sides, edges, corners, first, count, tile, tiles):
    tokens = tile * tiles
    total = 9 * tile

    def kernel(meta_ref, flag_ref, info_ref, qcol_ref, *refs):
        refs = list(refs)
        q_ref, k_ref, v_ref = refs[:3]
        del refs[:3]
        side_refs = [refs.pop(0) for _ in sides]
        edge_refs = [refs.pop(0) for _ in edges]
        corner_refs = [refs.pop(0) for _ in corners]
        if first:
            refs.pop(0)
        out_ref, key_buf, value_buf, col_mask = refs
        step = pl.program_id(0)
        place = step + first
        rad_f, rad_r, rad_c = meta_ref[1, place], meta_ref[2, place], meta_ref[3, place]

        @pl.when(step == 0)
        def _():
            gap = jnp.abs(qcol_ref[:, :1] - info_ref[0:1, :])
            for radius in range(2):
                col_mask[radius] = jnp.where(gap <= radius, 0.0, NEG_FILL)

        def lay(row, source_k, source_v, rows):
            key_buf[pl.ds(row, rows)] = source_k
            value_buf[pl.ds(row, rows)] = source_v

        def row_bias(band, at):
            off = jnp.zeros(band.shape, jnp.bool_)
            if at == 0:
                off = off | ((band == 0) & (flag_ref[2] == 0))
            if at == tiles - 1:
                off = off | ((band == 2) & (flag_ref[3] == 0))
            return off

        def side_bias(source):
            return ((source == 1) & (flag_ref[0] == 0)) | ((source == 2) & (flag_ref[1] == 0))

        def run(at, start, length, mask):
            rows = pl.ds(at * tile, tile)
            out_ref[rows, :] = attend(
                q_ref[rows, :], key_buf[pl.ds(start, length)], value_buf[pl.ds(start, length)], mask
            )

        if sides:

            @pl.when((rad_f > 0) & (rad_r > 0))
            def _():
                band, source = info_ref[1:2, :], info_ref[2:3, :]
                ends = [(edge_refs[0], edge_refs[1])] + [
                    (corner_refs[2 * i], corner_refs[2 * i + 1]) for i in range(2)
                ]
                for which in range(3):
                    low, high = ends[which]
                    lay(which * tile, low[0, 0], low[0, 1], tile)
                    lay((3 * (tiles + 1) + which) * tile, high[0, 0], high[0, 1], tile)
                    for at in range(tiles):
                        rows = pl.ds(at * tile, tile)
                        row = (3 * (at + 1) + which) * tile
                        if which == 0:
                            lay(row, k_ref[rows, :], v_ref[rows, :], tile)
                        else:
                            side = side_refs[which - 1]
                            lay(row, side[0, 0, rows, :], side[0, 1, rows, :], tile)
                col = col_mask[rad_c]
                for at in range(tiles):
                    bias = jnp.where(row_bias(band, at) | side_bias(source), NEG_FILL, 0.0)
                    run(at, 3 * at * tile, total, col + bias)

            @pl.when((rad_f > 0) & (rad_r == 0))
            def _():
                source = info_ref[3:4, : 3 * tile]
                for at in range(tiles):
                    rows = pl.ds(at * tile, tile)
                    lay(3 * at * tile, k_ref[rows, :], v_ref[rows, :], tile)
                    for which in (1, 2):
                        side = side_refs[which - 1]
                        lay((3 * at + which) * tile, side[0, 0, rows, :], side[0, 1, rows, :], tile)
                mask = col_mask[rad_c, :, : 3 * tile] + jnp.where(side_bias(source), NEG_FILL, 0.0)
                for at in range(tiles):
                    run(at, 3 * at * tile, 3 * tile, mask)

        @pl.when((rad_f == 0) & (rad_r > 0))
        def _():
            band = info_ref[3:4, : 3 * tile]
            lay(0, edge_refs[0][0, 0], edge_refs[0][0, 1], tile)
            lay(tile, k_ref[...], v_ref[...], tokens)
            lay(tile + tokens, edge_refs[1][0, 0], edge_refs[1][0, 1], tile)
            col = col_mask[rad_c, :, : 3 * tile]
            for at in range(tiles):
                bias = jnp.where(row_bias(band, at), NEG_FILL, 0.0)
                run(at, at * tile, 3 * tile, col + bias)

        @pl.when((rad_f == 0) & (rad_r == 0))
        def _():
            mask = col_mask[rad_c, :, :tile]
            for at in range(tiles):
                rows = pl.ds(at * tile, tile)
                out_ref[rows, :] = attend(q_ref[rows, :], k_ref[rows, :], v_ref[rows, :], mask)

    def columns(step, meta_ref, flag_ref):
        return (0, meta_ref[0, step + first])

    def by_place(limit):
        return lambda step, meta_ref, flag_ref: (jnp.minimum(step + first, limit - 1), 0, 0, 0)

    def by_slot(limit):
        return lambda step, meta_ref, flag_ref: (
            jnp.minimum(meta_ref[4, step + first], limit - 1), 0, 0, 0
        )

    def whole(step, meta_ref, flag_ref):
        return (0, 0)

    column_spec = pl.BlockSpec((tokens, HEAD_DIM), columns)
    in_specs = [pl.BlockSpec(key_info.shape, whole), pl.BlockSpec(query_col.shape, whole)]
    in_specs += [column_spec] * 3
    in_specs += [pl.BlockSpec((1,) + x.shape[1:], by_place(x.shape[0])) for x in sides]
    in_specs += [pl.BlockSpec((1,) + x.shape[1:], by_slot(x.shape[0])) for x in edges]
    in_specs += [pl.BlockSpec((1,) + x.shape[1:], by_place(x.shape[0])) for x in corners]
    operands = [key_info, query_col, *qkv[:3], *sides, *edges, *corners]
    aliases = {}
    if first:
        in_specs.append(pl.BlockSpec(memory_space=pl.ANY))
        operands.append(qkv[3])
        aliases = {2 + len(operands) - 1: 0}
    return pl.pallas_call(
        kernel,
        out_shape=jax.ShapeDtypeStruct(qkv[0].shape, jnp.bfloat16),
        grid_spec=pltpu.PrefetchScalarGridSpec(
            num_scalar_prefetch=2,
            grid=(count,),
            in_specs=in_specs,
            out_specs=column_spec,
            scratch_shapes=[
                pltpu.VMEM((3 * (tiles + 2) * tile, HEAD_DIM), jnp.bfloat16),
                pltpu.VMEM((3 * (tiles + 2) * tile, HEAD_DIM), jnp.bfloat16),
                pltpu.VMEM((2, tile, total), jnp.float32),
            ],
        ),
        input_output_aliases=aliases,
        compiler_params=pltpu.CompilerParams(vmem_limit_bytes=VMEM_BYTES),
    )(meta, flags, *operands)


def project(part, attended, own_weight, other_weight, block):
    tokens = attended.shape[0]
    depth, width = own_weight.shape

    def kernel(part_ref, own_ref, other_ref, own_w_ref, other_w_ref, out_ref):
        total = jnp.dot(own_ref[...], own_w_ref[...], preferred_element_type=jnp.float32)
        total += jnp.dot(other_ref[...], other_w_ref[...], preferred_element_type=jnp.float32)
        out_ref[...] = total.astype(out_ref.dtype)

    weight_spec = pl.BlockSpec((depth, block), lambda step, part_ref: (0, step))
    return pl.pallas_call(
        kernel,
        out_shape=jax.ShapeDtypeStruct((tokens, width), jnp.bfloat16),
        grid_spec=pltpu.PrefetchScalarGridSpec(
            num_scalar_prefetch=1,
            grid=(width // block,),
            in_specs=[
                pl.BlockSpec((tokens, depth), lambda step, part_ref: (0, part_ref[0])),
                pl.BlockSpec((tokens, depth), lambda step, part_ref: (0, 1 - part_ref[0])),
                weight_spec,
                weight_spec,
            ],
            out_specs=pl.BlockSpec((tokens, block), lambda step, part_ref: (0, step)),
        ),
        compiler_params=pltpu.CompilerParams(vmem_limit_bytes=VMEM_BYTES),
    )(part, attended, attended, own_weight, other_weight)


def on_device(queries, keys, values, out_weight, window_radii, frame_valid):
    _, rows_dev, col_total, width = queries.shape
    heads = width // HEAD_DIM
    tile = ROW_TILE * col_total
    tiles = rows_dev // ROW_TILE
    tokens = tile * tiles
    frame_pairs, height_total = lax.axis_size("frame"), lax.axis_size("height")
    frames = 2 * frame_pairs
    q, k, v = (x.reshape(tokens, width) for x in (queries, keys, values))
    outer_pairs = [(2 * i + 1, 2 * i + 2) for i in range(frame_pairs - 1)]
    outer_pairs += [(target, source) for source, target in outer_pairs]
    swap = [(0, 1), (1, 0)]
    down = [(i, i + 1) for i in range(height_total - 1)]
    up = [(i + 1, i) for i in range(height_total - 1)]

    part = lax.axis_index("head")
    frame = 2 * lax.axis_index("frame") + part
    height = lax.axis_index("height")

    index = jnp.arange(heads, dtype=jnp.int32)
    rad_f, rad_r, rad_c = window_radii[:, 0], window_radii[:, 1], window_radii[:, 2]
    rank_key = (2 * rad_f + rad_r) * heads - index
    edge_key = (2 * rad_r + rad_f) * heads - index
    rank = jnp.sum((rank_key[None, :] > rank_key[:, None]).astype(jnp.int32), axis=1)
    edge_rank = jnp.sum((edge_key[None, :] > edge_key[:, None]).astype(jnp.int32), axis=1)
    pick = (rank[None, :] == index[:, None]).astype(jnp.int32)
    features = jnp.stack((index, rad_f, rad_r, rad_c, edge_rank))
    meta = jnp.sum(features[:, None, :] * pick[None], axis=2)
    edge_order = jnp.sum((edge_rank[None, :] == index[:, None]) * index[None, :], axis=1)
    order = meta[0]

    inner, outer = frame + 1 - 2 * part, frame - 1 + 2 * part
    outer_ok = (outer >= 0) & (outer < frames) & (frame_valid[jnp.clip(outer, 0, frames - 1)] == 1)
    flags = jnp.stack(
        (frame_valid[inner] == 1, outer_ok, height > 0, height < height_total - 1)
    ).astype(jnp.int32)

    place = np.arange(9 * tile)
    key_info = np.zeros((8, 9 * tile), np.int32)
    key_info[0] = place % col_total // COL_TILE
    key_info[1] = place // (3 * tile)
    key_info[2] = place // tile % 3
    key_info[3] = place // tile
    query_col = np.broadcast_to((np.arange(tile) % col_total // COL_TILE)[:, None], (tile, 128))
    key_info, query_col = jnp.asarray(key_info), jnp.asarray(query_col.astype(np.int32))

    other_weight = lax.ppermute(out_weight, "head", swap)

    def finish(side_count, edge_count, corner_count):
        (packed,) = copy_columns(order, (k, v), side_count, [(0, tokens)])
        beyond = lax.ppermute(packed, GRID_AXES, outer_pairs)
        low, high = copy_columns(edge_order, (k, v), edge_count, [(0, tile), (tokens - tile, tile)])
        above = lax.ppermute(high, "height", down)
        below = lax.ppermute(low, "height", up)
        beside = lax.ppermute(packed, "head", swap)
        beside_above = lax.ppermute(above[:corner_count], "head", swap)
        beside_below = lax.ppermute(below[:corner_count], "head", swap)
        beyond_above = lax.ppermute(beyond[:corner_count, :, tokens - tile :], "height", down)
        beyond_below = lax.ppermute(beyond[:corner_count, :, :tile], "height", up)
        attended = attention(
            meta, flags, key_info, query_col, (q, k, v), (beside, beyond), (above, below),
            (beside_above, beside_below, beyond_above, beyond_below), 0, side_count, tile, tiles,
        )
        return project(part[None], attended, out_weight, other_weight, 512)

    projected = finish(heads, heads, heads)
    return projected.reshape(1, rows_dev, col_total, out_weight.shape[1])


def solution(mesh):
    return jax.shard_map(
        on_device,
        mesh=mesh,
        in_specs=(
            P(("frame", "head"), "height", None, None),
            P(("frame", "head"), "height", None, None),
            P(("frame", "head"), "height", None, None),
            P("head", None),
            P(),
            P(),
        ),
        out_specs=P(("frame", "head"), "height", None, None),
        check_vma=False,
    )
```

time: 457 us -> 342 us (0.75)
  the two profiles are of different devices: /device:TPU:1 before, /device:TPU:95 now
where the time goes in v1:
time: 342 us; the launch traced here: 341 us
  Pallas kernels  238 us (70%)
  waiting for transfers between devices  79 us (23%)
  starting transfers between devices  16.4 us (5%)
    pallas_call x2, Pallas kernels, copy_columns(): pl.pallas_call(kernel, out_shape=[jax.ShapeDtypeStruct((count, len(source...  182 us
    ppermute x1, waiting for transfers between devices, finish(): beyond = lax.ppermute(packed, GRID_AXES, outer_pairs)  38.8 us
    pallas_call x1, Pallas kernels, attention(): pl.pallas_call(kernel, out_shape=jax.ShapeDtypeStruct(qkv[0].shape, jnp.b...  37.2 us
    ppermute x1, waiting for transfers between devices, finish(): above = lax.ppermute(high, 'height', down)  18.8 us
    pallas_call x1, Pallas kernels, project(): pl.pallas_call(kernel, out_shape=jax.ShapeDtypeStruct((tokens, width), jn...  18.2 us
    ppermute x1, waiting for transfers between devices, finish(): beyond_below = lax.ppermute(beyond[:corner_count, :, :tile], 'height', up)  16.1 us
  transfers between devices with their start and end apart: 9, of which 4 were waited for; matrix products, arithmetic and copies ran while one was open for 2% of the time, Pallas kernels for 64%

profile of v1, /device:TPU:95, one launch (start us, length us, event | category | flops | bytes accessed | tf_op | source)
XLA Modules:
  0.0 340.9 jit_solution(6969635876282248853)
XLA Ops:
  0.0 0.7 collective-permute-start.8
  0.7 0.8 fusion.2
  1.4 0.8 subtract_bitcast_fusion.1
  2.2 0.2 convert_reduce_fusion
  2.5 0.2 multiply_reduce_fusion.meta_ref
  2.6 0.0 copy-start.2
  2.7 0.5 slice_bitcast_fusion.order_ref
  3.2 120.9 %shard_map.82 = bf16[20,2,384,128]{3,2,1,0:T(8,128)(2,1)} custom-call(s32[20]{0:T(128)} %slice_bitcast_fusion.order_ref, bf16[384,2560]{1,0:T(8,128)(2,1)} %bitcast.40, bf16[384,2560]{1,0:T(8,128)(2,1)} %bitcast.43), custom_call_target="tpu_custom_call" | custom-call | tf_op jit(solution)/shard_map/pallas_call | solution.py:46
  124.1 0.0 copy-done.2
  124.1 3.3 collective-permute-start.1
  127.4 0.1 collective-permute-start
  127.5 0.7 select_reduce_fusion.order_ref
  128.2 0.0 copy-start.3
  128.2 61.5 %shard_map.83 = (bf16[20,2,96,128]{3,2,1,0:T(8,128)(2,1)}, bf16[20,2,96,128]{3,2,1,0:T(8,128)(2,1)}) custom-call(s32[20]{0:T(128)} %select_reduce_fusion.order_ref, bf16[384,2560]{1,0:T(8,128)(2,1)} %bitcast.41, bf16[384,2560]{1,0:T(8,128)(2,1)} %bitcast.44), custom_call_target="tpu_custom_call" | custom-call | tf_op jit(solution)/shard_map/pallas_call | solution.py:46
  189.7 1.3 collective-permute-start.2
  191.0 5.0 %collective-permute-start.3 = (bf16[20,2,96,128]{3,2,1,0:T(8,128)(2,1)}, bf16[20,2,96,128]{3,2,1,0:T(8,128)(2,1)}, u32[]{:S(2)}, u32[]{:S(2)}) collective-permute-start(bf16[20,2,96,128]{3,2,1,0:T(8,128)(2,1)} %get-tuple-element.8), channel_id=1, source_target_pairs={{2,0},{4,2},{6,4},{8,6},{10,8},{12,10},{14,12},{3,1},{5,3},{7,5},{... | collective-permute-start | bytes 2949128 | tf_op jit(solution)/shard_map/ppermute | solution.py:298
  195.9 18.8 %collective-permute-done.2.refs_5_ = bf16[20,2,96,128]{3,2,1,0:T(8,128)(2,1)S(1)} collective-permute-done((bf16[20,2,96,128]{3,2,1,0:T(8,128)(2,1)}, bf16[20,2,96,128]{3,2,1,0:T(8,128)(2,1)S(1)}, u32[]{:S(2)}, u32[]{:S(2)}) %collective-permute-start.2) | collective-permute-done | bytes 983072 | tf_op jit(solution)/shard_map/ppermute | solution.py:297
  214.7 0.0 copy-start
  214.7 1.2 collective-permute-start.4
  215.9 0.0 collective-permute-done.3.refs_6_
  215.9 1.3 collective-permute-start.5
  217.2 38.8 %collective-permute-done.1.refs_4_ = bf16[20,2,384,128]{3,2,1,0:T(8,128)(2,1)} collective-permute-done((bf16[20,2,384,128]{3,2,1,0:T(8,128)(2,1)}, bf16[20,2,384,128]{3,2,1,0:T(8,128)(2,1)}, u32[]{:S(2)}, u32[]{:S(2)}) %collective-permute-start.1) | collective-permute-done | bytes 3932192 | tf_op jit(solution)/shard_map/ppermute | solution.py:295
  256.1 1.6 fusion.6
  257.7 2.2 collective-permute-start.7
  259.9 0.0 collective-permute-done.4.refs_7_
  259.9 0.0 copy-start.1
  259.9 1.3 collective-permute-start.6
  261.2 0.0 copy-done.1
  261.3 0.0 copy-done.3
  261.3 0.7 fusion.7
  263.3 0.7 add_convert_fusion.flag_ref
  264.0 0.0 collective-permute-done.5.refs_8_
  264.0 0.0 collective-permute-done.refs_3_
  264.0 16.1 %collective-permute-done.7.refs_10_ = bf16[20,2,96,128]{3,2,1,0:T(8,128)(2,1)} collective-permute-done((bf16[20,2,96,128]{3,2,1,0:T(8,128)(2,1)S(1)}, bf16[20,2,96,128]{3,2,1,0:T(8,128)(2,1)}, u32[]{:S(2)}, u32[]{:S(2)}) %collective-permute-start.7) | collective-permute-done | bytes 983072 | tf_op jit(solution)/shard_map/ppermute | solution.py:303
  280.1 5.3 %collective-permute-done.6.refs_9_ = bf16[20,2,96,128]{3,2,1,0:T(8,128)(2,1)} collective-permute-done((bf16[20,2,96,128]{3,2,1,0:T(8,128)(2,1)S(1)}, bf16[20,2,96,128]{3,2,1,0:T(8,128)(2,1)}, u32[]{:S(2)}, u32[]{:S(2)}) %collective-permute-start.6) | collective-permute-done | bytes 983072 | tf_op jit(solution)/shard_map/ppermute | solution.py:302
  285.4 0.0 copy-done
  285.4 37.2 %shard_map.84.own_ref.other_ref = bf16[384,2560]{1,0:T(8,128)(2,1)} custom-call(s32[5,20]{1,0:T(8,128)} %copy-done.2, s32[4]{0:T(128)} %add_convert_fusion.flag_ref, s32[8,864]{1,0:T(8,128)} %constant.38.clone.info_ref, s32[96,128]{1,0:T(8,128)} %constant.39.clone.qcol_ref, bf16[384,2560]{1,0:T(8,128)(2,1)} %bitcast.46, bf16[384,2560]{1,0:T(8,128)(2,1)} %bitcast.42, ...), custom_call_target="tpu_custom_call" | custom-call | tf_op jit(solution)/shard_map/pallas_call | solution.py:198
  322.6 0.0 collective-permute-done.8.other_w_ref
  322.6 18.2 %shard_map.85 = bf16[384,5120]{1,0:T(8,128)(2,1)} custom-call(s32[1]{0:T(128)} %bitcast.part_ref, bf16[384,2560]{1,0:T(8,128)(2,1)} %shard_map.84.own_ref.other_ref, bf16[384,2560]{1,0:T(8,128)(2,1)} %shard_map.84.own_ref.other_ref, bf16[1280,5120]{1,0:T(8,128)(2,1)} %own_w_ref.1, bf16[1280,5120]{1,0:T(8,128)(2,1)} %collective-permute-done.8.other_w_ref), custom_call_target="tpu_custom_call" | custom-call | tf_op jit(solution)/shard_map/pallas_call | solution.py:227
  (3 shorter events, 0.0 us)
Async XLA Ops:
  0.0 322.6 %collective-permute-start.8 = (bf16[1280,5120]{1,0:T(8,128)(2,1)}, bf16[1280,5120]{1,0:T(8,128)(2,1)}, u32[]{:S(2)}, u32[]{:S(2)}) collective-permute-start(bf16[1280,5120]{1,0:T(8,128)(2,1)} %own_w_ref.1), channel_id=1, source_target_pairs={{0,1},{1,0},{2,3},{3,2},{4,5},{5,4},{6,7},{7,6},{8,9},{9,8},{10,11... | collective-permute-start | bytes 39321608 | tf_op jit(solution)/shard_map/ppermute | solution.py:291
  2.6 121.4 %copy-start.2 = (s32[5,20]{1,0:T(8,128)}, s32[5,20]{1,0:T(8,128)S(1)}, u32[]{:S(2)}) copy-start(s32[5,20]{1,0:T(8,128)S(1)} %multiply_reduce_fusion.meta_ref) | copy-start | bytes 1204
  124.1 132.0 %collective-permute-start.1 = (bf16[20,2,384,128]{3,2,1,0:T(8,128)(2,1)}, bf16[20,2,384,128]{3,2,1,0:T(8,128)(2,1)}, u32[]{:S(2)}, u32[]{:S(2)}) collective-permute-start(bf16[20,2,384,128]{3,2,1,0:T(8,128)(2,1)} %shard_map.82), channel_id=1, source_target_pairs={{1,16},{17,32},{33,48},{49,64},{65,80},{81,96},{97,112},{16,1},{32... | collective-permute-start | bytes 11796488 | tf_op jit(solution)/shard_map/ppermute | solution.py:295
  127.4 136.6 %collective-permute-start = (bf16[20,2,384,128]{3,2,1,0:T(8,128)(2,1)}, bf16[20,2,384,128]{3,2,1,0:T(8,128)(2,1)}, u32[]{:S(2)}, u32[]{:S(2)}) collective-permute-start(bf16[20,2,384,128]{3,2,1,0:T(8,128)(2,1)} %shard_map.82), channel_id=1, source_target_pairs={{0,1},{1,0},{2,3},{3,2},{4,5},{5,4},{6,7},{7,6},{8,9},{9,8},{10,11... | collective-permute-start | bytes 11796488 | tf_op jit(solution)/shard_map/ppermute | solution.py:299
  128.2 133.1 %copy-start.3 = (s32[16]{0:T(128)S(1)}, s32[16]{0:T(128)}, u32[]{:S(2)}) copy-start(s32[16]{0:T(128)} %param.13) | copy-start | bytes 196
  189.7 25.0 %collective-permute-start.2 = (bf16[20,2,96,128]{3,2,1,0:T(8,128)(2,1)}, bf16[20,2,96,128]{3,2,1,0:T(8,128)(2,1)S(1)}, u32[]{:S(2)}, u32[]{:S(2)}) collective-permute-start(bf16[20,2,96,128]{3,2,1,0:T(8,128)(2,1)} %get-tuple-element.7), channel_id=1, source_target_pairs={{0,2},{2,4},{4,6},{6,8},{8,10},{10,12},{12,14},{1,3},{3,5},{5,7},{... | collective-permute-start | bytes 2949128 | tf_op jit(solution)/shard_map/ppermute | solution.py:297
  191.0 25.0 %collective-permute-start.3 = (bf16[20,2,96,128]{3,2,1,0:T(8,128)(2,1)}, bf16[20,2,96,128]{3,2,1,0:T(8,128)(2,1)}, u32[]{:S(2)}, u32[]{:S(2)}) collective-permute-start(bf16[20,2,96,128]{3,2,1,0:T(8,128)(2,1)} %get-tuple-element.8), channel_id=1, source_target_pairs={{2,0},{4,2},{6,4},{8,6},{10,8},{12,10},{14,12},{3,1},{5,3},{7,5},{... | collective-permute-start | bytes 2949128 | tf_op jit(solution)/shard_map/ppermute | solution.py:298
  214.7 70.7 %copy-start = (bf16[20,2,96,128]{3,2,1,0:T(8,128)(2,1)}, bf16[20,2,96,128]{3,2,1,0:T(8,128)(2,1)S(1)}, u32[]{:S(2)}) copy-start(bf16[20,2,96,128]{3,2,1,0:T(8,128)(2,1)S(1)} %collective-permute-done.2.refs_5_) | copy-start | bytes 2949124
  214.7 45.2 %collective-permute-start.4 = (bf16[20,2,96,128]{3,2,1,0:T(8,128)(2,1)S(1)}, bf16[20,2,96,128]{3,2,1,0:T(8,128)(2,1)S(1)}, u32[]{:S(2)}, u32[]{:S(2)}) collective-permute-start(bf16[20,2,96,128]{3,2,1,0:T(8,128)(2,1)S(1)} %collective-permute-done.2.refs_5_), channel_id=1, source_target_pairs={{0,1},{1,0},{2,3},{3,2},{4,5},{5,4},{6,7},{7,6},{8,9},{9,8},{10,11... | collective-permute-start | bytes 2949128 | tf_op jit(solution)/shard_map/ppermute | solution.py:300
  215.9 48.1 %collective-permute-start.5 = (bf16[20,2,96,128]{3,2,1,0:T(8,128)(2,1)}, bf16[20,2,96,128]{3,2,1,0:T(8,128)(2,1)}, u32[]{:S(2)}, u32[]{:S(2)}) collective-permute-start(bf16[20,2,96,128]{3,2,1,0:T(8,128)(2,1)} %collective-permute-done.3.refs_6_), channel_id=1, source_target_pairs={{0,1},{1,0},{2,3},{3,2},{4,5},{5,4},{6,7},{7,6},{8,9},{9,8},{10,11... | collective-permute-start | bytes 2949128 | tf_op jit(solution)/shard_map/ppermute | solution.py:301
  257.7 22.4 %collective-permute-start.7 = (bf16[20,2,96,128]{3,2,1,0:T(8,128)(2,1)S(1)}, bf16[20,2,96,128]{3,2,1,0:T(8,128)(2,1)}, u32[]{:S(2)}, u32[]{:S(2)}) collective-permute-start(bf16[20,2,96,128]{3,2,1,0:T(8,128)(2,1)S(1)} %get-tuple-element.9), channel_id=1, source_target_pairs={{2,0},{4,2},{6,4},{8,6},{10,8},{12,10},{14,12},{3,1},{5,3},{7,5},{... | collective-permute-start | bytes 2949128 | tf_op jit(solution)/shard_map/ppermute | solution.py:303
  259.9 1.3 copy-start.1
  259.9 25.5 %collective-permute-start.6 = (bf16[20,2,96,128]{3,2,1,0:T(8,128)(2,1)S(1)}, bf16[20,2,96,128]{3,2,1,0:T(8,128)(2,1)}, u32[]{:S(2)}, u32[]{:S(2)}) collective-permute-start(bf16[20,2,96,128]{3,2,1,0:T(8,128)(2,1)S(1)} %get-tuple-element.10), channel_id=1, source_target_pairs={{0,2},{2,4},{4,6},{6,8},{8,10},{10,12},{12,14},{1,3},{3,5},{5,7},{... | collective-permute-start | bytes 2949128 | tf_op jit(solution)/shard_map/ppermute | solution.py:302

commit v2 on v1

v2 whole, which is shorter than its diff:
```python
import functools
import math

import jax
import jax.numpy as jnp
import numpy as np
from jax import lax
from jax.experimental import pallas as pl
from jax.experimental.pallas import tpu as pltpu
from jax.sharding import PartitionSpec as P

HEAD_DIM = 128
ROW_TILE = 2
COL_TILE = 16
NEG_FILL = -1e30
GRID_AXES = ("frame", "head")
VMEM_BYTES = 56 * 1024 * 1024
SCALE = HEAD_DIM ** -0.5 * math.log2(math.e)


def pack_heads(order, sources, groups, tile, tiles):
    tokens, width = sources[0].shape

    def kernel(order_ref, *refs):
        ins, outs = refs[: len(sources)], refs[len(sources) :]
        for (first, count, which), out in zip(groups, outs):
            for at in range(count):
                columns = pl.ds(pl.multiple_of(order_ref[first + at] * HEAD_DIM, HEAD_DIM), HEAD_DIM)
                for index, source in enumerate(which):
                    out[at, index] = ins[source][:, columns]

    return pl.pallas_call(
        kernel,
        out_shape=[
            jax.ShapeDtypeStruct((count, len(which), tokens, HEAD_DIM), sources[0].dtype)
            for _, count, which in groups
        ],
        grid_spec=pltpu.PrefetchScalarGridSpec(
            num_scalar_prefetch=1,
            grid=(tiles,),
            in_specs=[pl.BlockSpec((tile, width), lambda step, order_ref: (step, 0)) for _ in sources],
            out_specs=[
                pl.BlockSpec((count, len(which), tile, HEAD_DIM), lambda step, order_ref: (0, 0, step, 0))
                for _, count, which in groups
            ],
        ),
        compiler_params=pltpu.CompilerParams(vmem_limit_bytes=VMEM_BYTES),
    )(order, *sources)


def pack_edges(order, keys, values, count, tile, tiles):
    width = keys.shape[1]

    def kernel(order_ref, *refs):
        ins, outs = refs[:4], refs[4:]
        for at in range(count):
            columns = pl.ds(pl.multiple_of(order_ref[at] * HEAD_DIM, HEAD_DIM), HEAD_DIM)
            for edge in range(2):
                for which in range(2):
                    outs[edge][at, which] = ins[2 * edge + which][:, columns]

    def rows(at):
        return pl.BlockSpec((tile, width), lambda step, order_ref: (at, 0))

    shape = (count, 2, tile, HEAD_DIM)
    return pl.pallas_call(
        kernel,
        out_shape=[jax.ShapeDtypeStruct(shape, keys.dtype)] * 2,
        grid_spec=pltpu.PrefetchScalarGridSpec(
            num_scalar_prefetch=1,
            grid=(1,),
            in_specs=[rows(0), rows(0), rows(tiles - 1), rows(tiles - 1)],
            out_specs=[pl.BlockSpec(shape, lambda step, order_ref: (0, 0, 0, 0))] * 2,
        ),
        compiler_params=pltpu.CompilerParams(vmem_limit_bytes=VMEM_BYTES),
    )(order, keys, values, keys, values)


def attend(query, keys, values, mask):
    scores = lax.dot_general(
        query, keys, (((1,), (1,)), ((), ())), preferred_element_type=jnp.float32
    )
    scores = scores * SCALE + mask
    highest = jnp.max(scores, axis=1, keepdims=True)
    expo = jnp.exp2(scores - highest)
    probs = expo * (1.0 / jnp.sum(expo, axis=1, keepdims=True))
    out = jnp.dot(probs.astype(jnp.bfloat16), values, preferred_element_type=jnp.float32)
    return out.astype(jnp.bfloat16)


def chunk(meta, flags, key_info, query_col, query, pair, sides, edges, corners, weights, total_in,
          first, count, block, last, tile, tiles):
    tokens = tile * tiles
    span = 9 * tile
    width = weights[0].shape[1]
    blocks = width // block

    def kernel(meta_ref, flag_ref, info_ref, qcol_ref, *refs):
        refs = list(refs)
        q_ref, pair_ref = refs.pop(0), refs.pop(0)
        side_refs = [refs.pop(0) for _ in sides]
        edge_refs = [refs.pop(0) for _ in edges]
        corner_refs = [refs.pop(0) for _ in corners]
        weight_refs = [refs.pop(0) for _ in weights]
        total_ref = None if total_in is None else refs.pop(0)
        out_ref, key_buf, value_buf, col_mask, attended, weight_buf, sem = refs
        step = pl.program_id(0)
        place = jnp.minimum(step, count - 1) + first
        rad_f, rad_r, rad_c = meta_ref[1, place], meta_ref[2, place], meta_ref[3, place]

        def weight_copy(at, source):
            row = pl.multiple_of(meta_ref[6, first + at] * HEAD_DIM, HEAD_DIM)
            return pltpu.make_async_copy(
                source.at[pl.ds(row, HEAD_DIM), :],
                weight_buf.at[pl.ds(at * HEAD_DIM, HEAD_DIM), :],
                sem.at[at],
            )

        @pl.when(step == 0)
        def _():
            for at in range(count):
                own = meta_ref[5, first + at] == flag_ref[4]

                @pl.when(own)
                def _():
                    weight_copy(at, weight_refs[0]).start()

                @pl.when(jnp.logical_not(own))
                def _():
                    weight_copy(at, weight_refs[1]).start()

            gap = jnp.abs(qcol_ref[:, :1] - info_ref[0:1, :])
            for radius in range(2):
                col_mask[radius] = jnp.where(gap <= radius, 0.0, NEG_FILL)

        def lay(row, source_k, source_v, rows):
            key_buf[pl.ds(row, rows)] = source_k
            value_buf[pl.ds(row, rows)] = source_v

        def row_off(band, at):
            off = jnp.zeros(band.shape, jnp.bool_)
            if at == 0:
                off = off | ((band == 0) & (flag_ref[2] == 0))
            if at == tiles - 1:
                off = off | ((band == 2) & (flag_ref[3] == 0))
            return off

        def side_off(source):
            return ((source == 1) & (flag_ref[0] == 0)) | ((source == 2) & (flag_ref[1] == 0))

        def run(at, start, length, mask):
            rows = pl.ds(at * tile, tile)
            attended[step, rows, :] = attend(
                q_ref[0, 0, rows, :], key_buf[pl.ds(start, length)], value_buf[pl.ds(start, length)], mask
            )

        attending = step < count
        if sides:

            @pl.when(attending & (rad_f > 0) & (rad_r > 0))
            def _():
                band, source = info_ref[1:2, :], info_ref[2:3, :]
                ends = [(edge_refs[0], edge_refs[1])] + [
                    (corner_refs[2 * i], corner_refs[2 * i + 1]) for i in range(2)
                ]
                for which, body in enumerate([pair_ref] + side_refs):
                    low, high = ends[which]
                    lay(which * tile, low[0, 0], low[0, 1], tile)
                    lay((3 * (tiles + 1) + which) * tile, high[0, 0], high[0, 1], tile)
                    for at in range(tiles):
                        rows = pl.ds(at * tile, tile)
                        lay((3 * (at + 1) + which) * tile, body[0, 0, rows, :], body[0, 1, rows, :], tile)
                col = col_mask[rad_c]
                for at in range(tiles):
                    bias = jnp.where(row_off(band, at) | side_off(source), NEG_FILL, 0.0)
                    run(at, 3 * at * tile, span, col + bias)

            @pl.when(attending & (rad_f > 0) & (rad_r == 0))
            def _():
                source = info_ref[3:4, : 3 * tile]
                for which, body in enumerate([pair_ref] + side_refs):
                    for at in range(tiles):
                        rows = pl.ds(at * tile, tile)
                        lay((3 * at + which) * tile, body[0, 0, rows, :], body[0, 1, rows, :], tile)
                mask = col_mask[rad_c, :, : 3 * tile] + jnp.where(side_off(source), NEG_FILL, 0.0)
                for at in range(tiles):
                    run(at, 3 * at * tile, 3 * tile, mask)

        @pl.when(attending & (rad_f == 0) & (rad_r > 0))
        def _():
            band = info_ref[3:4, : 3 * tile]
            lay(0, edge_refs[0][0, 0], edge_refs[0][0, 1], tile)
            lay(tile, pair_ref[0, 0], pair_ref[0, 1], tokens)
            lay(tile + tokens, edge_refs[1][0, 0], edge_refs[1][0, 1], tile)
            col = col_mask[rad_c, :, : 3 * tile]
            for at in range(tiles):
                run(at, at * tile, 3 * tile, col + jnp.where(row_off(band, at), NEG_FILL, 0.0))

        @pl.when(attending & (rad_f == 0) & (rad_r == 0))
        def _():
            mask = col_mask[rad_c, :, :tile]
            for at in range(tiles):
                rows = pl.ds(at * tile, tile)
                attended[step, rows, :] = attend(
                    q_ref[0, 0, rows, :], pair_ref[0, 0, rows, :], pair_ref[0, 1, rows, :], mask
                )

        @pl.when(step == count)
        def _():
            for at in range(count):
                weight_copy(at, weight_refs[0]).wait()

        @pl.when(step >= count)
        def _():
            columns = pl.ds(pl.multiple_of((step - count) * block, block), block)
            left = jnp.concatenate([attended[at] for at in range(count)], axis=1)
            total = jnp.dot(left, weight_buf[:, columns], preferred_element_type=jnp.float32)
            if total_ref is not None:
                total += total_ref[...]
            out_ref[...] = total.astype(out_ref.dtype)

    def own_place(step):
        return jnp.minimum(step, count - 1)

    def whole(step, meta_ref, flag_ref):
        return (0, 0)

    def output_block(step, meta_ref, flag_ref):
        return (0, jnp.maximum(step - count, 0))

    def by_place(x):
        return pl.BlockSpec(
            (1,) + x.shape[1:], lambda step, meta_ref, flag_ref: (own_place(step), 0, 0, 0)
        )

    def by_slot(x):
        return pl.BlockSpec(
            (1,) + x.shape[1:],
            lambda step, meta_ref, flag_ref: (meta_ref[4, own_place(step) + first], 0, 0, 0),
        )

    in_specs = [pl.BlockSpec(key_info.shape, whole), pl.BlockSpec(query_col.shape, whole)]
    in_specs.append(
        pl.BlockSpec(
            (1,) + query.shape[1:], lambda step, meta_ref, flag_ref: (own_place(step) + first, 0, 0, 0)
        )
    )
    in_specs.append(by_place(pair))
    in_specs += [by_place(x) for x in sides]
    in_specs += [by_slot(x) for x in edges]
    in_specs += [by_place(x) for x in corners]
    in_specs += [pl.BlockSpec(memory_space=pl.ANY)] * 2
    operands = [key_info, query_col, query, pair, *sides, *edges, *corners, *weights]
    if total_in is not None:
        in_specs.append(pl.BlockSpec((tokens, block), output_block))
        operands.append(total_in)
    return pl.pallas_call(
        kernel,
        out_shape=jax.ShapeDtypeStruct((tokens, width), jnp.bfloat16 if last else jnp.float32),
        grid_spec=pltpu.PrefetchScalarGridSpec(
            num_scalar_prefetch=2,
            grid=(count + blocks,),
            in_specs=in_specs,
            out_specs=pl.BlockSpec((tokens, block), output_block),
            scratch_shapes=[
                pltpu.VMEM((3 * (tiles + 2) * tile, HEAD_DIM), jnp.bfloat16),
                pltpu.VMEM((3 * (tiles + 2) * tile, HEAD_DIM), jnp.bfloat16),
                pltpu.VMEM((2, tile, span), jnp.float32),
                pltpu.VMEM((count, tokens, HEAD_DIM), jnp.bfloat16),
                pltpu.VMEM((count * HEAD_DIM, width), jnp.bfloat16),
                pltpu.SemaphoreType.DMA((count,)),
            ],
        ),
        compiler_params=pltpu.CompilerParams(vmem_limit_bytes=VMEM_BYTES),
    )(meta, flags, *operands)


def on_device(queries, keys, values, out_weight, window_radii, frame_valid):
    _, rows_dev, col_total, width = queries.shape
    heads = width // HEAD_DIM
    tile = ROW_TILE * col_total
    tiles = rows_dev // ROW_TILE
    tokens = tile * tiles
    frame_pairs, height_total = lax.axis_size("frame"), lax.axis_size("height")
    frames = 2 * frame_pairs
    q, k, v = (x.reshape(tokens, width) for x in (queries, keys, values))
    outer_pairs = [(2 * i + 1, 2 * i + 2) for i in range(frame_pairs - 1)]
    outer_pairs += [(target, source) for source, target in outer_pairs]
    swap = [(0, 1), (1, 0)]
    down = [(i, i + 1) for i in range(height_total - 1)]
    up = [(i + 1, i) for i in range(height_total - 1)]

    part = lax.axis_index("head")
    frame = 2 * lax.axis_index("frame") + part
    height = lax.axis_index("height")

    index = jnp.arange(heads, dtype=jnp.int32)
    rad_f, rad_r, rad_c = window_radii[:, 0], window_radii[:, 1], window_radii[:, 2]
    rank_key = (2 * rad_f + rad_r) * heads - index
    edge_key = (2 * rad_r + rad_f) * heads - index
    rank = jnp.sum((rank_key[None, :] > rank_key[:, None]).astype(jnp.int32), axis=1)
    edge_rank = jnp.sum((edge_key[None, :] > edge_key[:, None]).astype(jnp.int32), axis=1)
    pick = (rank[None, :] == index[:, None]).astype(jnp.int32)
    half = heads // 2
    features = jnp.stack((index, rad_f, rad_r, rad_c, edge_rank, index // half, index % half))
    meta = jnp.sum(features[:, None, :] * pick[None], axis=2)
    edge_order = jnp.sum((edge_rank[None, :] == index[:, None]) * index[None, :], axis=1)
    order = meta[0]
    n_side, n_edge, n_corner = jnp.sum(rad_f), jnp.sum(rad_r), jnp.sum(rad_f * rad_r)

    inner, outer = frame + 1 - 2 * part, frame - 1 + 2 * part
    outer_ok = (outer >= 0) & (outer < frames) & (frame_valid[jnp.clip(outer, 0, frames - 1)] == 1)
    flags = jnp.stack(
        (frame_valid[inner] == 1, outer_ok, height > 0, height < height_total - 1, part)
    ).astype(jnp.int32)

    place = np.arange(9 * tile)
    key_info = np.zeros((8, 9 * tile), np.int32)
    key_info[0] = place % col_total // COL_TILE
    key_info[1] = place // (3 * tile)
    key_info[2] = place // tile % 3
    key_info[3] = place // tile
    query_col = np.broadcast_to((np.arange(tile) % col_total // COL_TILE)[:, None], (tile, 128))
    key_info, query_col = jnp.asarray(key_info), jnp.asarray(query_col.astype(np.int32))

    def exchange_edges(count):
        def call(k, v, edge_order):
            low, high = pack_edges(edge_order, k, v, count, tile, tiles)
            got = lax.ppermute(high, "height", down), lax.ppermute(low, "height", up)
            return tuple(jnp.pad(x, ((0, heads - count),) + ((0, 0),) * 3) for x in got)

        return call

    def exchange_corners(size, count):
        def call(beyond):
            if count == 0:
                return (jnp.zeros((size, 2, tile, HEAD_DIM), beyond.dtype),) * 2
            got = (
                lax.ppermute(beyond[:count, :, tokens - tile :], "height", down),
                lax.ppermute(beyond[:count, :, :tile], "height", up),
            )
            return tuple(jnp.pad(x, ((0, size - count),) + ((0, 0),) * 3) for x in got)

        return call

    def finish(side_count):
        def call(q, k, v, out_weight):
            sizes = split_sides(side_count)
            starts = [sum(sizes[:i]) for i in range(len(sizes))]
            rest = heads - side_count
            packed, beyond, beside = [], [], []
            if sizes:
                packed = pack_heads(order, (k, v), [(s, n, (0, 1)) for s, n in zip(starts, sizes)], tile, tiles)
                beyond = [lax.ppermute(x, GRID_AXES, outer_pairs) for x in packed]
                beside = [lax.ppermute(x, "head", swap) for x in packed]
            other_weight = lax.ppermute(out_weight, "head", swap)
            groups = [(0, heads, (0,))] + ([(side_count, rest, (1, 2))] if rest else [])
            ordered = pack_heads(order, (q, k, v), groups, tile, tiles)
            query = ordered[0]
            levels = [4, 8, 10, 12, 16, heads]
            level = sum((n_edge > x).astype(jnp.int32) for x in levels[:-1])
            edges = lax.switch(level, [exchange_edges(x) for x in levels], k, v, edge_order)
            weights = (out_weight, other_weight)
            total = None
            if rest:
                total = chunk(
                    meta, flags, key_info, query_col, query, ordered[1], (), edges, (), weights, total,
                    side_count, rest, 512, not sizes, tile, tiles,
                )
            for i, (start, size) in enumerate(zip(starts, sizes)):
                near = [lax.ppermute(x[start : start + size], "head", swap) for x in edges]
                levels = sorted({0, (size + 1) // 2, size})
                level = sum((n_corner - start > x).astype(jnp.int32) for x in levels[:-1])
                far = lax.switch(level, [exchange_corners(size, x) for x in levels], beyond[i])
                total = chunk(
                    meta, flags, key_info, query_col, query, packed[i], (beside[i], beyond[i]), edges,
                    (*near, *far), weights, total, start, size, 512, i == len(sizes) - 1, tile, tiles,
                )
            return total

        return call

    side_levels = list(range(0, heads + 1, 2))
    level = sum((n_side > x).astype(jnp.int32) for x in side_levels[:-1])
    projected = lax.switch(level, [finish(x) for x in side_levels], q, k, v, out_weight)
    return projected.reshape(1, rows_dev, col_total, out_weight.shape[1])


def split_sides(count):
    if count <= 2:
        return [count] if count else []
    if count <= 4:
        return [count - 2, 2]
    return [count - 4, 2, 2]


def solution(mesh):
    return jax.shard_map(
        on_device,
        mesh=mesh,
        in_specs=(
            P(("frame", "head"), "height", None, None),
            P(("frame", "head"), "height", None, None),
            P(("frame", "head"), "height", None, None),
            P("head", None),
            P(),
            P(),
        ),
        out_specs=P(("frame", "head"), "height", None, None),
        check_vma=False,
    )
```

time: 342 us -> 232 us (0.68)
  the two profiles are of different devices: /device:TPU:95 before, /device:TPU:71 now
where the time goes in v2:
time: 232 us; the launch traced here: 229 us
  Pallas kernels  95.6 us (41%)
  loops' own time  46.8 us (20%)
  starting transfers between devices  32 us (14%)
  waiting for transfers between devices  31.8 us (14%)
  local copies, waits for them, and re-layouts  10.4 us (4%)
  between operations  8.42 us (4%)
  other arithmetic  3.61 us (2%)
    pallas_call x4, Pallas kernels, chunk(): pl.pallas_call(kernel, out_shape=jax.ShapeDtypeStruct((tokens, width), jn...  82.5 us
    another operation x1, loops' own time, on_device(): lax.switch(level, [finish(x) for x in side_levels], q, k, v, out_weight)  46.6 us
    ppermute x2, waiting for transfers between devices, call(): got = (lax.ppermute(high, 'height', down), lax.ppermute(low, 'height', up))  16.3 us
    ppermute x2, waiting for transfers between devices, call(): lax.ppermute(beyond[:count, :, :tile], 'height', up)  10.8 us
    ppermute x3, starting transfers between devices, call(): beyond = [lax.ppermute(x, GRID_AXES, outer_pairs) for x in packed]  10.5 us
    pallas_call x2, Pallas kernels, pack_heads(): pl.pallas_call(kernel, out_shape=[jax.ShapeDtypeStruct((count, len(which)...  10.2 us
    ppermute x2, starting transfers between devices, call(): lax.ppermute(beyond[:count, :, :tile], 'height', up)  6.73 us
    ppermute x2, starting transfers between devices, call(): got = (lax.ppermute(high, 'height', down), lax.ppermute(low, 'height', up))  6.65 us
  transfers between devices with their start and end apart: 19, of which 8 were waited for; matrix products, arithmetic and copies ran while one was open for 3% of the time, Pallas kernels for 36%

profile of v2, /device:TPU:71, one launch (start us, length us, event | category | flops | bytes accessed | tf_op | source)
XLA Modules:
  0.0 228.7 jit_solution(1024720663919525453)
XLA Ops:
  0.0 1.4 fusion.73
  2.8 0.1 stack.43
  2.8 1.5 slice_bitcast_fusion.1
  4.3 0.8 iota_subtract_fusion.1
  5.1 0.2 convert_reduce_fusion
  5.3 0.4 multiply_reduce_fusion.10
  5.8 0.1 slice_reduce_fusion
  5.9 0.1 select_reduce_fusion
  12.5 213.8 %conditional.39 = (bf16[1,8,48,5120]{3,2,1,0:T(8,128)(2,1)S(1)}) conditional(s32[]{:T(128)} %clamp.117, (s32[20]{0:T(128)S(1)}, bf16[384,2560]{1,0:T(8,128)(2,1)}, bf16[384,2560]{1,0:T(8,128)(2,1)}, bf16[384,2560]{1,0:T(8,128)(2,1)}, s32[]{:T(128)}, /*index=5*/s32[20]{0:T(128)S(1)}, bf16[1280,5120]{1,0:T(8,128)(2,1)}, ...), branch_computations={%region_7.14_spmd, %region_14.24_spmd, %region_24.37_spmd, %region... | conditional | flops 74 | bytes 130595624 | solution.py:385
  30.2 0.0 copy-start.2
  30.2 0.8 collective-permute-start.259
  30.9 4.6 %branch_3_fun.22 = (bf16[2,2,384,128]{3,2,1,0:T(8,128)(2,1)}, bf16[2,2,384,128]{3,2,1,0:T(8,128)(2,1)}, bf16[2,2,384,128]{3,2,1,0:T(8,128)(2,1)}) custom-call(s32[20]{0:T(128)S(1)} %get-tuple-element.909.order_ref, bf16[384,2560]{1,0:T(8,128)(2,1)} %get-tuple-element.911.refs_1_.refs_0_, bf16[384,2560]{1,0:T(8,128)(2,1)} %get-tuple-element.912.refs_2_.refs_1_), custom_call_target="tpu_custom_call" | custom-call | tf_op jit(solution)/shard_map/cond/branch_3_fun/pallas_call | solution.py:32
  35.6 3.1 %collective-permute-start.265 = (bf16[2,2,384,128]{3,2,1,0:T(8,128)(2,1)}, bf16[2,2,384,128]{3,2,1,0:T(8,128)(2,1)S(1)}, u32[]{:S(2)}, u32[]{:S(2)}) collective-permute-start(bf16[2,2,384,128]{3,2,1,0:T(8,128)(2,1)} %get-tuple-element.926.refs_1_), channel_id=1, source_target_pairs={{1,16},{17,32},{33,48},{49,64},{65,80},{81,96},{97,112},{16,1},{32... | collective-permute-start | bytes 1179656 | tf_op jit(solution)/shard_map/cond/branch_3_fun/ppermute | solution.py:354
  38.7 2.5 %collective-permute-start.261 = (bf16[2,2,384,128]{3,2,1,0:T(8,128)(2,1)}, bf16[2,2,384,128]{3,2,1,0:T(8,128)(2,1)S(1)}, u32[]{:S(2)}, u32[]{:S(2)}) collective-permute-start(bf16[2,2,384,128]{3,2,1,0:T(8,128)(2,1)} %get-tuple-element.923.refs_1_), channel_id=1, source_target_pairs={{1,16},{17,32},{33,48},{49,64},{65,80},{81,96},{97,112},{16,1},{32... | collective-permute-start | bytes 1179656 | tf_op jit(solution)/shard_map/cond/branch_3_fun/ppermute | solution.py:354
  44.2 28.1 %conditional.6 = (bf16[20,2,96,128]{3,2,1,0:T(8,128)(2,1)}, bf16[20,2,96,128]{3,2,1,0:T(8,128)(2,1)}) conditional(s32[]{:T(128)} %clamp.84, (s32[20]{0:T(128)S(1)}, bf16[384,2560]{1,0:T(8,128)(2,1)S(1)}, bf16[384,2560]{1,0:T(8,128)(2,1)}) %tuple.940, (s32[20]{0:T(128)S(1)}, bf16[384,2560]{1,0:T(8,128)(2,1)S(1)}, ...), branch_computations={%region_38.38_spmd, %region_39.39_spmd, %region_40.40_spmd, %regio... | conditional | bytes 9830500 | solution.py:362
  44.3 3.0 %branch_3_fun.20 = (bf16[12,2,96,128]{3,2,1,0:T(8,128)(2,1)}, bf16[12,2,96,128]{3,2,1,0:T(8,128)(2,1)}) custom-call(s32[20]{0:T(128)S(1)} %get-tuple-element.890.order_ref, bf16[384,2560]{1,0:T(8,128)(2,1)S(1)} %get-tuple-element.891.refs_0_.refs_2_, bf16[384,2560]{1,0:T(8,128)(2,1)} %get-tuple-element.892.refs_1_.refs_3_, ...), custom_call_target="tpu_custom_call" | custom-call | tf_op jit(solution)/shard_map/cond/branch_3_fun/cond/branch_3_fun/pallas_call | solution.py:66
  47.2 4.7 %collective-permute-start.43 = (bf16[12,2,96,128]{3,2,1,0:T(8,128)(2,1)}, bf16[12,2,96,128]{3,2,1,0:T(8,128)(2,1)S(1)}, u32[]{:S(2)}, u32[]{:S(2)}) collective-permute-start(bf16[12,2,96,128]{3,2,1,0:T(8,128)(2,1)} %get-tuple-element.893), channel_id=1, source_target_pairs={{0,2},{2,4},{4,6},{6,8},{8,10},{10,12},{12,14},{1,3},{3,5},{5,7},{... | collective-permute-start | bytes 1769480 | tf_op jit(solution)/shard_map/cond/branch_3_fun/cond/branch_3_fun/ppermute | solution.py:329
  52.0 1.9 collective-permute-start.44
  53.9 10.1 %collective-permute-done.43 = bf16[12,2,96,128]{3,2,1,0:T(8,128)(2,1)S(1)} collective-permute-done((bf16[12,2,96,128]{3,2,1,0:T(8,128)(2,1)}, bf16[12,2,96,128]{3,2,1,0:T(8,128)(2,1)S(1)}, u32[]{:S(2)}, u32[]{:S(2)}) %collective-permute-start.43) | collective-permute-done | bytes 589856 | tf_op jit(solution)/shard_map/cond/branch_3_fun/cond/branch_3_fun/ppermute | solution.py:329
  64.0 1.1 pad.383
  65.1 6.2 %collective-permute-done.44 = bf16[12,2,96,128]{3,2,1,0:T(8,128)(2,1)S(1)} collective-permute-done((bf16[12,2,96,128]{3,2,1,0:T(8,128)(2,1)}, bf16[12,2,96,128]{3,2,1,0:T(8,128)(2,1)S(1)}, u32[]{:S(2)}, u32[]{:S(2)}) %collective-permute-start.44) | collective-permute-done | bytes 589856 | tf_op jit(solution)/shard_map/cond/branch_3_fun/cond/branch_3_fun/ppermute | solution.py:329
  71.3 1.1 pad.384
  72.4 4.9 %collective-permute-start.256 = (bf16[2,2,384,128]{3,2,1,0:T(8,128)(2,1)}, bf16[2,2,384,128]{3,2,1,0:T(8,128)(2,1)S(1)}, u32[]{:S(2)}, u32[]{:S(2)}) collective-permute-start(bf16[2,2,384,128]{3,2,1,0:T(8,128)(2,1)} %get-tuple-element.914.refs_1_), channel_id=1, source_target_pairs={{1,16},{17,32},{33,48},{49,64},{65,80},{81,96},{97,112},{16,1},{32... | collective-permute-start | bytes 1179656 | tf_op jit(solution)/shard_map/cond/branch_3_fun/ppermute | solution.py:354
  77.3 0.6 multiply_reduce_fusion.2
  79.2 0.0 collective-permute-done.265.refs_3_
  79.2 12.0 %conditional.9 = (bf16[2,2,96,128]{3,2,1,0:T(8,128)(2,1)}, bf16[2,2,96,128]{3,2,1,0:T(8,128)(2,1)}) conditional(s32[]{:T(128)} %clamp.87, () %tuple.457, bf16[2,2,384,128]{3,2,1,0:T(8,128)(2,1)S(1)} %collective-permute-done.265.refs_3_, bf16[2,2,384,128]{3,2,1,0:T(8,128)(2,1)S(1)} %collective-permute-done.265.refs_3_), branch_computations={%region_50.50_spmd, %region_51.51_spmd, %region_52.52_spmd} | conditional | bytes 1179744 | solution.py:374
  79.3 1.9 collective-permute-start.160
  81.2 3.4 %collective-permute-start.161 = (bf16[2,2,96,128]{3,2,1,0:T(8,128)(2,1)S(1)}, bf16[2,2,96,128]{3,2,1,0:T(8,128)(2,1)}, u32[]{:S(2)}, u32[]{:S(2)}) collective-permute-start(bf16[2,2,96,128]{3,2,1,0:T(8,128)(2,1)S(1)} %get-tuple-element.1680), channel_id=1, source_target_pairs={{2,0},{4,2},{6,4},{8,6},{10,8},{12,10},{14,12},{3,1},{5,3},{7,5},{... | collective-permute-start | bytes 294920 | tf_op jit(solution)/shard_map/cond/branch_3_fun/cond/branch_2_fun/ppermute | solution.py:340
  84.6 1.4 collective-permute-done.160
  86.0 5.2 %collective-permute-done.161 = bf16[2,2,96,128]{3,2,1,0:T(8,128)(2,1)} collective-permute-done((bf16[2,2,96,128]{3,2,1,0:T(8,128)(2,1)S(1)}, bf16[2,2,96,128]{3,2,1,0:T(8,128)(2,1)}, u32[]{:S(2)}, u32[]{:S(2)}) %collective-permute-start.161) | collective-permute-done | bytes 98336 | tf_op jit(solution)/shard_map/cond/branch_3_fun/cond/branch_2_fun/ppermute | solution.py:340
  91.2 0.8 collective-permute-start.264
  92.7 0.0 collective-permute-done.261.refs_3_
  92.7 12.0 %conditional.8 = (bf16[2,2,96,128]{3,2,1,0:T(8,128)(2,1)}, bf16[2,2,96,128]{3,2,1,0:T(8,128)(2,1)}) conditional(s32[]{:T(128)} %clamp.86, () %tuple.456, bf16[2,2,384,128]{3,2,1,0:T(8,128)(2,1)S(1)} %collective-permute-done.261.refs_3_, bf16[2,2,384,128]{3,2,1,0:T(8,128)(2,1)S(1)} %collective-permute-done.261.refs_3_), branch_computations={%region_47.47_spmd, %region_48.48_spmd, %region_49.49_spmd} | conditional | bytes 1179744 | solution.py:374
  92.8 1.9 collective-permute-start.156
  94.7 3.4 %collective-permute-start.157 = (bf16[2,2,96,128]{3,2,1,0:T(8,128)(2,1)S(1)}, bf16[2,2,96,128]{3,2,1,0:T(8,128)(2,1)}, u32[]{:S(2)}, u32[]{:S(2)}) collective-permute-start(bf16[2,2,96,128]{3,2,1,0:T(8,128)(2,1)S(1)} %get-tuple-element.1676), channel_id=1, source_target_pairs={{2,0},{4,2},{6,4},{8,6},{10,8},{12,10},{14,12},{3,1},{5,3},{7,5},{... | collective-permute-start | bytes 294920 | tf_op jit(solution)/shard_map/cond/branch_3_fun/cond/branch_2_fun/ppermute | solution.py:340
  98.1 1.1 collective-permute-done.156
  99.2 5.5 %collective-permute-done.157 = bf16[2,2,96,128]{3,2,1,0:T(8,128)(2,1)} collective-permute-done((bf16[2,2,96,128]{3,2,1,0:T(8,128)(2,1)S(1)}, bf16[2,2,96,128]{3,2,1,0:T(8,128)(2,1)}, u32[]{:S(2)}, u32[]{:S(2)}) %collective-permute-start.157) | collective-permute-done | bytes 98336 | tf_op jit(solution)/shard_map/cond/branch_3_fun/cond/branch_2_fun/ppermute | solution.py:340
  104.7 0.8 collective-permute-start.260
  106.2 0.0 copy-start.14
  106.2 0.0 copy-start.25
  106.2 0.0 collective-permute-done.256.refs_3_
  106.2 1.3 conditional.7
  106.2 0.7 broadcast.258
  106.9 0.7 broadcast.258.clone
  107.5 0.0 collective-permute-start.255
  107.5 1.0 fusion.58
  108.6 0.6 collective-permute-start.266
  109.1 1.0 fusion.57
  110.2 0.3 collective-permute-start.267
  110.4 1.1 collective-permute-done.267.refs_7_
  111.6 0.6 copy-done.54
  112.2 0.2 collective-permute-start.262
  112.4 1.1 collective-permute-done.262.refs_6_
  113.5 0.2 collective-permute-start.263
  113.7 0.3 collective-permute-start.257
  114.0 0.4 collective-permute-start.258
  114.4 5.6 %branch_3_fun.21 = (bf16[20,1,384,128]{3,2,1,0:T(8,128)(2,1)}, bf16[14,2,384,128]{3,2,1,0:T(8,128)(2,1)}) custom-call(s32[20]{0:T(128)S(1)} %get-tuple-element.909.order_ref, bf16[384,2560]{1,0:T(8,128)(2,1)} %get-tuple-element.910.refs_0_, bf16[384,2560]{1,0:T(8,128)(2,1)S(1)} %copy-done.2, bf16[384,2560]{1,0:T(8,128)(2,1)} %get-tuple-element.912.refs_2_.refs_1_), custom_call_target="tpu_custom_call" | custom-call | tf_op jit(solution)/shard_map/cond/branch_3_fun/pallas_call | solution.py:32
  120.0 0.7 copy.34.meta_ref
  120.7 37.3 %branch_3_fun.23.refs_12_ = f32[384,5120]{1,0:T(8,128)} custom-call(s32[7,20]{1,0:T(8,128)} %copy.34.meta_ref, s32[5]{0:T(128)S(1)} %get-tuple-element.906.flag_ref, s32[8,864]{1,0:T(8,128)S(1)} %copy-done.25, s32[96,128]{1,0:T(8,128)S(1)} %copy-done.14, bf16[20,1,384,128]{3,2,1,0:T(8,128)(2,1)} %get-tuple-element.913.refs_0_, ...), custom_call_target="tpu_custom_call" | custom-call | tf_op jit(solution)/shard_map/cond/branch_3_fun/pallas_call | solution.py:257
  158.0 15.9 %branch_3_fun.24.refs_12_ = f32[384,5120]{1,0:T(8,128)} custom-call(s32[7,20]{1,0:T(8,128)} %copy.34.meta_ref, s32[5]{0:T(128)S(1)} %get-tuple-element.906.flag_ref, s32[8,864]{1,0:T(8,128)S(1)} %copy-done.25, s32[96,128]{1,0:T(8,128)S(1)} %copy-done.14, bf16[20,1,384,128]{3,2,1,0:T(8,128)(2,1)} %get-tuple-element.913.refs_0_, ...), custom_call_target="tpu_custom_call" | custom-call | tf_op jit(solution)/shard_map/cond/branch_3_fun/pallas_call | solution.py:257
  173.9 15.9 %branch_3_fun.25.refs_12_ = f32[384,5120]{1,0:T(8,128)} custom-call(s32[7,20]{1,0:T(8,128)} %copy.34.meta_ref, s32[5]{0:T(128)S(1)} %get-tuple-element.906.flag_ref, s32[8,864]{1,0:T(8,128)S(1)} %copy-done.25, s32[96,128]{1,0:T(8,128)S(1)} %copy-done.14, bf16[20,1,384,128]{3,2,1,0:T(8,128)(2,1)} %get-tuple-element.913.refs_0_, ...), custom_call_target="tpu_custom_call" | custom-call | tf_op jit(solution)/shard_map/cond/branch_3_fun/pallas_call | solution.py:257
  189.9 13.3 %branch_3_fun.26 = bf16[384,5120]{1,0:T(8,128)(2,1)S(1)} custom-call(s32[7,20]{1,0:T(8,128)} %copy.34.meta_ref, s32[5]{0:T(128)S(1)} %get-tuple-element.906.flag_ref, s32[8,864]{1,0:T(8,128)S(1)} %copy-done.25, s32[96,128]{1,0:T(8,128)S(1)} %copy-done.14, bf16[20,1,384,128]{3,2,1,0:T(8,128)(2,1)} %get-tuple-element.913.refs_0_, ...), custom_call_target="tpu_custom_call" | custom-call | tf_op jit(solution)/shard_map/cond/branch_3_fun/pallas_call | solution.py:257
  226.3 0.0 copy-start.33
  226.3 1.9 copy-done.33
  (22 shorter events, 0.1 us)
Async XLA Ops:
  30.2 14.1 %copy-start.2 = (bf16[384,2560]{1,0:T(8,128)(2,1)S(1)}, bf16[384,2560]{1,0:T(8,128)(2,1)}, u32[]{:S(2)}) copy-start(bf16[384,2560]{1,0:T(8,128)(2,1)} %get-tuple-element.911.refs_1_.refs_0_) | copy-start | bytes 5898244 | tf_op jit(solution)/shard_map/cond
  30.2 83.8 %collective-permute-start.259 = (bf16[1280,5120]{1,0:T(8,128)(2,1)}, bf16[1280,5120]{1,0:T(8,128)(2,1)}, u32[]{:S(2)}, u32[]{:S(2)}) collective-permute-start(bf16[1280,5120]{1,0:T(8,128)(2,1)} %get-tuple-element.922.refs_4_.refs_10_), channel_id=1, source_target_pairs={{0,1},{1,0},{2,3},{3,2},{4,5},{5,4},{6,7},{7,6},{8,9},{9,8},{10,11... | collective-permute-start | bytes 39321608 | tf_op jit(solution)/shard_map/cond/branch_3_fun/ppermute | solution.py:356
  35.6 43.7 %collective-permute-start.265 = (bf16[2,2,384,128]{3,2,1,0:T(8,128)(2,1)}, bf16[2,2,384,128]{3,2,1,0:T(8,128)(2,1)S(1)}, u32[]{:S(2)}, u32[]{:S(2)}) collective-permute-start(bf16[2,2,384,128]{3,2,1,0:T(8,128)(2,1)} %get-tuple-element.926.refs_1_), channel_id=1, source_target_pairs={{1,16},{17,32},{33,48},{49,64},{65,80},{81,96},{97,112},{16,1},{32... | collective-permute-start | bytes 1179656 | tf_op jit(solution)/shard_map/cond/branch_3_fun/ppermute | solution.py:354
  38.7 54.1 %collective-permute-start.261 = (bf16[2,2,384,128]{3,2,1,0:T(8,128)(2,1)}, bf16[2,2,384,128]{3,2,1,0:T(8,128)(2,1)S(1)}, u32[]{:S(2)}, u32[]{:S(2)}) collective-permute-start(bf16[2,2,384,128]{3,2,1,0:T(8,128)(2,1)} %get-tuple-element.923.refs_1_), channel_id=1, source_target_pairs={{1,16},{17,32},{33,48},{49,64},{65,80},{81,96},{97,112},{16,1},{32... | collective-permute-start | bytes 1179656 | tf_op jit(solution)/shard_map/cond/branch_3_fun/ppermute | solution.py:354
  47.2 16.8 %collective-permute-start.43 = (bf16[12,2,96,128]{3,2,1,0:T(8,128)(2,1)}, bf16[12,2,96,128]{3,2,1,0:T(8,128)(2,1)S(1)}, u32[]{:S(2)}, u32[]{:S(2)}) collective-permute-start(bf16[12,2,96,128]{3,2,1,0:T(8,128)(2,1)} %get-tuple-element.893), channel_id=1, source_target_pairs={{0,2},{2,4},{4,6},{6,8},{8,10},{10,12},{12,14},{1,3},{3,5},{5,7},{... | collective-permute-start | bytes 1769480 | tf_op jit(solution)/shard_map/cond/branch_3_fun/cond/branch_3_fun/ppermute | solution.py:329
  52.0 19.3 %collective-permute-start.44 = (bf16[12,2,96,128]{3,2,1,0:T(8,128)(2,1)}, bf16[12,2,96,128]{3,2,1,0:T(8,128)(2,1)S(1)}, u32[]{:S(2)}, u32[]{:S(2)}) collective-permute-start(bf16[12,2,96,128]{3,2,1,0:T(8,128)(2,1)} %get-tuple-element.894), channel_id=1, source_target_pairs={{2,0},{4,2},{6,4},{8,6},{10,8},{12,10},{14,12},{3,1},{5,3},{7,5},{... | collective-permute-start | bytes 1769480 | tf_op jit(solution)/shard_map/cond/branch_3_fun/cond/branch_3_fun/ppermute | solution.py:329
  72.4 33.9 %collective-permute-start.256 = (bf16[2,2,384,128]{3,2,1,0:T(8,128)(2,1)}, bf16[2,2,384,128]{3,2,1,0:T(8,128)(2,1)S(1)}, u32[]{:S(2)}, u32[]{:S(2)}) collective-permute-start(bf16[2,2,384,128]{3,2,1,0:T(8,128)(2,1)} %get-tuple-element.914.refs_1_), channel_id=1, source_target_pairs={{1,16},{17,32},{33,48},{49,64},{65,80},{81,96},{97,112},{16,1},{32... | collective-permute-start | bytes 1179656 | tf_op jit(solution)/shard_map/cond/branch_3_fun/ppermute | solution.py:354
  79.3 6.7 %collective-permute-start.160 = (bf16[2,2,96,128]{3,2,1,0:T(8,128)(2,1)S(1)}, bf16[2,2,96,128]{3,2,1,0:T(8,128)(2,1)}, u32[]{:S(2)}, u32[]{:S(2)}) collective-permute-start(bf16[2,2,96,128]{3,2,1,0:T(8,128)(2,1)S(1)} %get-tuple-element.1681), channel_id=1, source_target_pairs={{0,2},{2,4},{4,6},{6,8},{8,10},{10,12},{12,14},{1,3},{3,5},{5,7},{... | collective-permute-start | bytes 294920 | tf_op jit(solution)/shard_map/cond/branch_3_fun/cond/branch_2_fun/ppermute | solution.py:339
  81.2 10.0 %collective-permute-start.161 = (bf16[2,2,96,128]{3,2,1,0:T(8,128)(2,1)S(1)}, bf16[2,2,96,128]{3,2,1,0:T(8,128)(2,1)}, u32[]{:S(2)}, u32[]{:S(2)}) collective-permute-start(bf16[2,2,96,128]{3,2,1,0:T(8,128)(2,1)S(1)} %get-tuple-element.1680), channel_id=1, source_target_pairs={{2,0},{4,2},{6,4},{8,6},{10,8},{12,10},{14,12},{3,1},{5,3},{7,5},{... | collective-permute-start | bytes 294920 | tf_op jit(solution)/shard_map/cond/branch_3_fun/cond/branch_2_fun/ppermute | solution.py:340
  91.2 22.5 %collective-permute-start.264 = (bf16[2,2,384,128]{3,2,1,0:T(8,128)(2,1)}, bf16[2,2,384,128]{3,2,1,0:T(8,128)(2,1)}, u32[]{:S(2)}, u32[]{:S(2)}) collective-permute-start(bf16[2,2,384,128]{3,2,1,0:T(8,128)(2,1)} %get-tuple-element.926.refs_1_), channel_id=1, source_target_pairs={{0,1},{1,0},{2,3},{3,2},{4,5},{5,4},{6,7},{7,6},{8,9},{9,8},{10,11... | collective-permute-start | bytes 1179656 | tf_op jit(solution)/shard_map/cond/branch_3_fun/ppermute | solution.py:355
  92.8 6.4 %collective-permute-start.156 = (bf16[2,2,96,128]{3,2,1,0:T(8,128)(2,1)S(1)}, bf16[2,2,96,128]{3,2,1,0:T(8,128)(2,1)}, u32[]{:S(2)}, u32[]{:S(2)}) collective-permute-start(bf16[2,2,96,128]{3,2,1,0:T(8,128)(2,1)S(1)} %get-tuple-element.1677), channel_id=1, source_target_pairs={{0,2},{2,4},{4,6},{6,8},{8,10},{10,12},{12,14},{1,3},{3,5},{5,7},{... | collective-permute-start | bytes 294920 | tf_op jit(solution)/shard_map/cond/branch_3_fun/cond/branch_2_fun/ppermute | solution.py:339
  94.7 10.0 %collective-permute-start.157 = (bf16[2,2,96,128]{3,2,1,0:T(8,128)(2,1)S(1)}, bf16[2,2,96,128]{3,2,1,0:T(8,128)(2,1)}, u32[]{:S(2)}, u32[]{:S(2)}) collective-permute-start(bf16[2,2,96,128]{3,2,1,0:T(8,128)(2,1)S(1)} %get-tuple-element.1676), channel_id=1, source_target_pairs={{2,0},{4,2},{6,4},{8,6},{10,8},{12,10},{14,12},{3,1},{5,3},{7,5},{... | collective-permute-start | bytes 294920 | tf_op jit(solution)/shard_map/cond/branch_3_fun/cond/branch_2_fun/ppermute | solution.py:340
  104.7 69.2 %collective-permute-start.260 = (bf16[2,2,384,128]{3,2,1,0:T(8,128)(2,1)}, bf16[2,2,384,128]{3,2,1,0:T(8,128)(2,1)}, u32[]{:S(2)}, u32[]{:S(2)}) collective-permute-start(bf16[2,2,384,128]{3,2,1,0:T(8,128)(2,1)} %get-tuple-element.923.refs_1_), channel_id=1, source_target_pairs={{0,1},{1,0},{2,3},{3,2},{4,5},{5,4},{6,7},{7,6},{8,9},{9,8},{10,11... | collective-permute-start | bytes 1179656 | tf_op jit(solution)/shard_map/cond/branch_3_fun/ppermute | solution.py:355
  106.2 14.5 %copy-start.14 = (s32[96,128]{1,0:T(8,128)S(1)}, s32[96,128]{1,0:T(8,128)}, u32[]{:S(2)}) copy-start(s32[96,128]{1,0:T(8,128)} %get-tuple-element.908.qcol_ref) | copy-start | bytes 147460 | tf_op jit(solution)/shard_map/cond
  106.2 14.5 %copy-start.25 = (s32[8,864]{1,0:T(8,128)S(1)}, s32[8,864]{1,0:T(8,128)}, u32[]{:S(2)}) copy-start(s32[8,864]{1,0:T(8,128)} %get-tuple-element.907.info_ref) | copy-start | bytes 82948 | tf_op jit(solution)/shard_map/cond
  107.5 82.4 %collective-permute-start.255 = (bf16[2,2,384,128]{3,2,1,0:T(8,128)(2,1)}, bf16[2,2,384,128]{3,2,1,0:T(8,128)(2,1)}, u32[]{:S(2)}, u32[]{:S(2)}) collective-permute-start(bf16[2,2,384,128]{3,2,1,0:T(8,128)(2,1)} %get-tuple-element.914.refs_1_), channel_id=1, source_target_pairs={{0,1},{1,0},{2,3},{3,2},{4,5},{5,4},{6,7},{7,6},{8,9},{9,8},{10,11... | collective-permute-start | bytes 1179656 | tf_op jit(solution)/shard_map/cond/branch_3_fun/ppermute | solution.py:355
  108.6 1.6 collective-permute-start.266
  110.2 4.3 %copy-start.51 = (bf16[2,2,96,128]{3,2,1,0:T(8,128)(2,1)}, bf16[2,2,96,128]{3,2,1,0:T(8,128)(2,1)S(1)}, u32[]{:S(2)}) copy-start(bf16[2,2,96,128]{3,2,1,0:T(8,128)(2,1)S(1)} %collective-permute-done.266.refs_6_) | copy-start | bytes 294916 | tf_op jit(solution)/shard_map/cond
  110.2 1.4 collective-permute-start.267
  111.6 0.6 copy-start.54
  112.2 1.3 collective-permute-start.262
  113.5 0.9 copy-start.52
  113.5 60.4 %collective-permute-start.263 = (bf16[2,2,96,128]{3,2,1,0:T(8,128)(2,1)S(1)}, bf16[2,2,96,128]{3,2,1,0:T(8,128)(2,1)}, u32[]{:S(2)}, u32[]{:S(2)}) collective-permute-start(bf16[2,2,96,128]{3,2,1,0:T(8,128)(2,1)S(1)} %get-tuple-element.1771), channel_id=1, source_target_pairs={{0,1},{1,0},{2,3},{3,2},{4,5},{5,4},{6,7},{7,6},{8,9},{9,8},{10,11... | collective-permute-start | bytes 294920 | tf_op jit(solution)/shard_map/cond/branch_3_fun/ppermute | solution.py:371
  113.7 76.2 %collective-permute-start.257 = (bf16[2,2,96,128]{3,2,1,0:T(8,128)(2,1)S(1)}, bf16[2,2,96,128]{3,2,1,0:T(8,128)(2,1)}, u32[]{:S(2)}, u32[]{:S(2)}) collective-permute-start(bf16[2,2,96,128]{3,2,1,0:T(8,128)(2,1)S(1)} %get-tuple-element.1775), channel_id=1, source_target_pairs={{0,1},{1,0},{2,3},{3,2},{4,5},{5,4},{6,7},{7,6},{8,9},{9,8},{10,11... | collective-permute-start | bytes 294920 | tf_op jit(solution)/shard_map/cond/branch_3_fun/ppermute | solution.py:371
  114.0 75.9 %collective-permute-start.258 = (bf16[2,2,96,128]{3,2,1,0:T(8,128)(2,1)S(1)}, bf16[2,2,96,128]{3,2,1,0:T(8,128)(2,1)}, u32[]{:S(2)}, u32[]{:S(2)}) collective-permute-start(bf16[2,2,96,128]{3,2,1,0:T(8,128)(2,1)S(1)} %get-tuple-element.1772), channel_id=1, source_target_pairs={{0,1},{1,0},{2,3},{3,2},{4,5},{5,4},{6,7},{7,6},{8,9},{9,8},{10,11... | collective-permute-start | bytes 294920 | tf_op jit(solution)/shard_map/cond/branch_3_fun/ppermute | solution.py:371
  226.3 1.9 copy-start.33
